TPU v7x, 1024 devices: a whole 4x4x32 slice. The times are simulated.
1024 devices in a mesh: row: 64 (over z, x_lo), col: 16 (over x_hi, y, core).
Axes of the slice: x: 4 (x_hi: 2, x_lo: 2; x = x_hi * 2 + x_lo), y: 4, z: 32, core: 2. Of those that a mesh axis runs over, the one named last changes fastest.
Arguments:
- image_feats: bfloat16 [262144, 768], P(('row', 'col')), may hold values from -24 to 24
- text_emb: bfloat16 [262144, 768], P(('row', 'col')), may hold values from -0.21582031 to 0.21582031
- head_weight: bfloat16 [768, 768], replicated, may hold values from -0.21875 to 0.21875
- partner: int32 [262144], P(('row', 'col')), may hold values from 0 to 262143, as said below
Outputs:
- row_loss: float32 [262144], P(('row', 'col'))
- feat_grad: bfloat16 [262144, 768], P(('row', 'col'))
- text_grad: float32 [262144, 768], P(('row', 'col'))
- head_grad: float32 [768, 768], P('row', 'col')
Inputs may be any that keep to these rules, and one draw needn't show every extreme that they name: Each image row's positive text row lies in a text block at loop distance at most 2 from its own block: partner[i] // 256 differs from i // 256 by at most 2 modulo 262144 / 256.
All inputs are finite; a program needn't handle non-finite values.
Results may differ from a plain program's by a relative error of at most 0.017.
Values may be sent and summed in bfloat16 or wider, within the bound.
No kernel may reach another device: no remote copies, remote signals or barrier semaphores. Data moves between devices by JAX's collectives and lax.ppermute only.
A program may use at most 32 MiB of HBM per device.

v0:
```python
import jax
import jax.numpy as jnp
from jax import lax
from jax.sharding import PartitionSpec as P

HALF = 2


TEMP = 10.0
BIAS = -4.0


def passed_along(block, axis, distance):
    devices = range(lax.axis_size(axis))
    route = [((i - distance) % len(devices), i) for i in devices]
    return lax.ppermute(block, axis, route)


def block_slope(unit_b, partner, text_rows, owner):
    rows = text_rows.shape[0]
    cols = owner * rows + jnp.arange(rows, dtype=jnp.int32)
    label = jnp.where(partner[:, None] == cols[None, :], 1.0, -1.0).astype(jnp.float32)
    logit = (
        TEMP
        * lax.dot_general(
            unit_b, text_rows, (((1,), (1,)), ((), ())), preferred_element_type=jnp.float32
        )
        + BIAS
    )
    loss = jnp.sum(jax.nn.softplus(-label * logit), axis=1)
    slope = (-label * jax.nn.sigmoid(-label * logit)).astype(jnp.bfloat16)
    return (loss, slope)


def image_term(slope, text_rows):
    return TEMP * jnp.dot(slope, text_rows, preferred_element_type=jnp.float32)


def text_term(slope, unit_b):
    return TEMP * lax.dot_general(
        slope, unit_b, (((0,), (0,)), ((), ())), preferred_element_type=jnp.float32
    )


def block_terms(unit_b, partner, text_rows, owner):
    loss, slope = block_slope(unit_b, partner, text_rows, owner)
    return (loss, image_term(slope, text_rows), text_term(slope, unit_b))


def local(image_feats, text_emb, head_weight, partner):
    count = lax.axis_size(("row", "col"))
    here = lax.axis_index(("row", "col"))
    proj = jnp.dot(image_feats, head_weight, preferred_element_type=jnp.float32)
    norm = jnp.sqrt(jnp.sum(proj * proj, axis=1, keepdims=True) + 1e-06)
    unit = proj / norm
    unit_b = unit.astype(jnp.bfloat16)
    row_loss = jnp.zeros((image_feats.shape[0],), jnp.float32)
    unit_grad = jnp.zeros(proj.shape, jnp.float32)
    current = passed_along(text_emb, ("row", "col"), -HALF)
    accum = jnp.zeros(proj.shape, jnp.float32)
    for step in range(2 * HALF + 1):
        owner = (here + HALF - step) % count
        loss, image_part, text_part = block_terms(unit_b, partner, current, owner)
        row_loss = row_loss + loss
        unit_grad = unit_grad + image_part
        accum = accum + text_part
        if step < 2 * HALF:
            current = passed_along(current, ("row", "col"), 1)
            accum = passed_along(accum.astype(jnp.bfloat16), ("row", "col"), 1).astype(accum.dtype)
    text_grad = passed_along(accum.astype(jnp.bfloat16), ("row", "col"), -HALF).astype(accum.dtype)
    inner = jnp.sum(unit * unit_grad, axis=1, keepdims=True)
    proj_grad = ((unit_grad - unit * inner) / norm).astype(jnp.bfloat16)
    feat_grad = lax.dot_general(
        proj_grad, head_weight, (((1,), (1,)), ((), ())), preferred_element_type=jnp.float32
    ).astype(jnp.bfloat16)
    head_terms = lax.dot_general(
        image_feats, proj_grad, (((0,), (0,)), ((), ())), preferred_element_type=jnp.float32
    )
    partial_rows = lax.psum_scatter(head_terms, "row", scatter_dimension=0, tiled=True)
    head_grad = lax.psum_scatter(
        partial_rows.astype(jnp.bfloat16), "col", scatter_dimension=1, tiled=True
    ).astype(jnp.float32)
    return (row_loss, feat_grad, text_grad, head_grad)


def solution(mesh):
    return jax.shard_map(
        local,
        mesh=mesh,
        in_specs=(P(("row", "col"), None), P(("row", "col"), None), P(), P(("row", "col"))),
        out_specs=(
            P(("row", "col")),
            P(("row", "col"), None),
            P(("row", "col"), None),
            P("row", "col"),
        ),
        check_vma=False,
    )
```

profile of v0, /device:TPU:1, one launch (start us, length us, event | category | flops | bytes accessed | tf_op | source)
XLA Modules:
  0.0 489.3 jit_solution(6676560356184904284)
XLA Ops:
  7.2 24.0 %collective-permute-start = (bf16[256,768]{1,0:T(8,128)(2,1)}, bf16[256,768]{1,0:T(8,128)(2,1)S(1)}, u32[]{:S(2)}, u32[]{:S(2)}) collective-permute-start(bf16[256,768]{1,0:T(8,128)(2,1)} %param.5), channel_id=1, source_target_pairs={{2,0},{3,1},{4,2},{5,3},{6,4},{7,5},{8,6},{9,7},{10,8},{11,9},{12,... | collective-permute-start | bytes 1179656 | tf_op jit(solution)/shard_map/ppermute | solution.py:16
  31.3 1.6 multiply_reduce_fusion.1
  33.0 1.3 dynamic-slice
  34.9 0.1 fusion.18
  35.0 4.3 collective-permute-done
  39.3 1.9 collective-permute-start.1
  41.2 0.5 fusion.12
  41.7 0.3 fusion.1
  42.1 1.9 collective-permute-start.5
  44.0 0.4 fusion.17
  44.4 1.5 collective-permute-done.1
  45.9 4.4 collective-permute-start.2
  50.3 0.5 fusion.13
  50.8 0.3 add_convert_fusion.3
  51.2 3.7 collective-permute-start.6
  54.9 0.4 convolution_add_fusion.3
  55.3 3.2 collective-permute-done.2
  58.5 1.9 collective-permute-start.3
  60.4 0.5 fusion.14
  60.9 0.3 convolution_multiply_fusion.2
  61.2 1.8 collective-permute-done.6
  63.0 0.1 add_convert_fusion.2
  63.1 1.9 collective-permute-start.7
  65.0 0.4 convolution_add_fusion.2
  65.4 7.5 %collective-permute-done.3 = bf16[256,768]{1,0:T(8,128)(2,1)S(1)} collective-permute-done((bf16[256,768]{1,0:T(8,128)(2,1)S(1)}, bf16[256,768]{1,0:T(8,128)(2,1)S(1)}, u32[]{:S(2)}, u32[]{:S(2)}) %collective-permute-start.3) | collective-permute-done | bytes 393248 | tf_op jit(solution)/shard_map/ppermute | solution.py:16
  73.0 1.9 collective-permute-start.4
  74.9 0.5 fusion.15
  75.4 0.3 convolution_multiply_fusion.1
  75.7 1.9 collective-permute-done.7
  77.7 1.9 collective-permute-start.8
  79.6 0.4 convolution_add_fusion.1
  80.0 7.5 %collective-permute-done.4 = bf16[256,768]{1,0:T(8,128)(2,1)S(1)} collective-permute-done((bf16[256,768]{1,0:T(8,128)(2,1)S(1)}, bf16[256,768]{1,0:T(8,128)(2,1)S(1)}, u32[]{:S(2)}, u32[]{:S(2)}) %collective-permute-start.4) | collective-permute-done | bytes 393248 | tf_op jit(solution)/shard_map/ppermute | solution.py:16
  87.5 1.1 fusion.16
  88.6 0.3 convolution_multiply_fusion
  88.9 3.3 collective-permute-done.8
  92.2 0.8 add_convert_fusion
  93.1 12.2 %collective-permute-start.9 = (bf16[256,768]{1,0:T(8,128)(2,1)}, bf16[256,768]{1,0:T(8,128)(2,1)}, u32[]{:S(2)}, u32[]{:S(2)}) collective-permute-start(bf16[256,768]{1,0:T(8,128)(2,1)} %add_convert_fusion), channel_id=1, source_target_pairs={{2,0},{3,1},{4,2},{5,3},{6,4},{7,5},{8,6},{9,7},{10,8},{11,9},{12,... | collective-permute-start | bytes 1179656 | tf_op jit(solution)/shard_map/ppermute | solution.py:16
  105.3 0.5 multiply_reduce_fusion
  105.8 0.2 divide_convert_fusion
  106.0 0.7 copy-done.1
  106.8 0.5 convolution_bitcast_fusion
  107.3 212.7 %all-reduce.2 = bf16[768,768]{0,1:T(8,128)(2,1)} all-reduce(f32[768,768]{0,1:T(8,128)S(1)} %convolution_bitcast_fusion), channel_id=2, replica_groups=mesh['row'=64,'col'=16] {'row'}, use_global_device_ids=true, to_apply=%region_7.8.clone | all-reduce | flops 589824 | bytes 3538944
  320.0 1.8 dynamic-slice_convert_fusion
  321.8 2.2 convolution_convert_fusion
  324.0 0.6 add_add_fusion
  324.6 154.5 %reduce-scatter.3.cloned.1.call-done = bf16[12,48]{0,1:T(8,128)(2,1)} async-done(((bf16[12,768]{0,1:T(8,128)(2,1)}), bf16[12,48]{0,1:T(8,128)(2,1)}) %reduce-scatter.3.cloned.1.call-update) | async-done | bytes 1168 | tf_op jit(solution)/shard_map/reduce_scatter | solution.py:80
  479.1 1.4 copy.9
  480.5 1.9 convert_element_type.77
  (20 shorter events, 0.2 us)
Async XLA Ops:
  7.2 24.1 %copy-start = (bf16[768,768]{1,0:T(8,128)(2,1)S(1)}, bf16[768,768]{1,0:T(8,128)(2,1)}, u32[]{:S(2)}) copy-start(bf16[768,768]{1,0:T(8,128)(2,1)} %param.6) | copy-start | bytes 3538948
  7.2 471.9 %reduce-scatter.3.cloned.1.call-start = ((), (), s32[]{:S(2)}) async-start(), calls=%async_computation.1 | async-start | bytes 208896 | tf_op jit(solution)/shard_map/reduce_scatter | solution.py:80
  7.2 32.1 %collective-permute-start = (bf16[256,768]{1,0:T(8,128)(2,1)}, bf16[256,768]{1,0:T(8,128)(2,1)S(1)}, u32[]{:S(2)}, u32[]{:S(2)}) collective-permute-start(bf16[256,768]{1,0:T(8,128)(2,1)} %param.5), channel_id=1, source_target_pairs={{2,0},{3,1},{4,2},{5,3},{6,4},{7,5},{8,6},{9,7},{10,8},{11,9},{12,... | collective-permute-start | bytes 1179656 | tf_op jit(solution)/shard_map/ppermute | solution.py:16
  32.9 8.4 %copy-start.3 = (s32[256]{0:T(256)S(1)}, s32[256]{0:T(256)}, u32[]{:S(2)}) copy-start(s32[256]{0:T(256)} %param.7) | copy-start | bytes 3076
  39.3 6.6 %collective-permute-start.1 = (bf16[256,768]{1,0:T(8,128)(2,1)S(1)}, bf16[256,768]{1,0:T(8,128)(2,1)S(1)}, u32[]{:S(2)}, u32[]{:S(2)}) collective-permute-start(bf16[256,768]{1,0:T(8,128)(2,1)S(1)} %collective-permute-done), channel_id=1, source_target_pairs={{1023,0},{0,1},{1,2},{2,3},{3,4},{4,5},{5,6},{6,7},{7,8},{8,9},{9,... | collective-permute-start | bytes 1179656 | tf_op jit(solution)/shard_map/ppermute | solution.py:16
  42.1 8.7 %collective-permute-start.5 = (bf16[256,768]{1,0:T(8,128)(2,1)S(1)}, bf16[256,768]{1,0:T(8,128)(2,1)S(1)}, u32[]{:S(2)}, u32[]{:S(2)}) collective-permute-start(bf16[256,768]{1,0:T(8,128)(2,1)S(1)} %fusion.1), channel_id=1, source_target_pairs={{1023,0},{0,1},{1,2},{2,3},{3,4},{4,5},{5,6},{6,7},{7,8},{8,9},{9,... | collective-permute-start | bytes 1179656 | tf_op jit(solution)/shard_map/ppermute | solution.py:16
  45.9 12.6 %collective-permute-start.2 = (bf16[256,768]{1,0:T(8,128)(2,1)S(1)}, bf16[256,768]{1,0:T(8,128)(2,1)S(1)}, u32[]{:S(2)}, u32[]{:S(2)}) collective-permute-start(bf16[256,768]{1,0:T(8,128)(2,1)S(1)} %collective-permute-done.1), channel_id=1, source_target_pairs={{1023,0},{0,1},{1,2},{2,3},{3,4},{4,5},{5,6},{6,7},{7,8},{8,9},{9,... | collective-permute-start | bytes 1179656 | tf_op jit(solution)/shard_map/ppermute | solution.py:16
  51.2 11.9 %collective-permute-start.6 = (bf16[256,768]{1,0:T(8,128)(2,1)S(1)}, bf16[256,768]{1,0:T(8,128)(2,1)S(1)}, u32[]{:S(2)}, u32[]{:S(2)}) collective-permute-start(bf16[256,768]{1,0:T(8,128)(2,1)S(1)} %add_convert_fusion.3), channel_id=1, source_target_pairs={{1023,0},{0,1},{1,2},{2,3},{3,4},{4,5},{5,6},{6,7},{7,8},{8,9},{9,... | collective-permute-start | bytes 1179656 | tf_op jit(solution)/shard_map/ppermute | solution.py:16
  58.5 14.5 %collective-permute-start.3 = (bf16[256,768]{1,0:T(8,128)(2,1)S(1)}, bf16[256,768]{1,0:T(8,128)(2,1)S(1)}, u32[]{:S(2)}, u32[]{:S(2)}) collective-permute-start(bf16[256,768]{1,0:T(8,128)(2,1)S(1)} %collective-permute-done.2), channel_id=1, source_target_pairs={{1023,0},{0,1},{1,2},{2,3},{3,4},{4,5},{5,6},{6,7},{7,8},{8,9},{9,... | collective-permute-start | bytes 1179656 | tf_op jit(solution)/shard_map/ppermute | solution.py:16
  63.1 14.5 %collective-permute-start.7 = (bf16[256,768]{1,0:T(8,128)(2,1)S(1)}, bf16[256,768]{1,0:T(8,128)(2,1)S(1)}, u32[]{:S(2)}, u32[]{:S(2)}) collective-permute-start(bf16[256,768]{1,0:T(8,128)(2,1)S(1)} %add_convert_fusion.2), channel_id=1, source_target_pairs={{1023,0},{0,1},{1,2},{2,3},{3,4},{4,5},{5,6},{6,7},{7,8},{8,9},{9,... | collective-permute-start | bytes 1179656 | tf_op jit(solution)/shard_map/ppermute | solution.py:16
  73.0 14.5 %collective-permute-start.4 = (bf16[256,768]{1,0:T(8,128)(2,1)S(1)}, bf16[256,768]{1,0:T(8,128)(2,1)S(1)}, u32[]{:S(2)}, u32[]{:S(2)}) collective-permute-start(bf16[256,768]{1,0:T(8,128)(2,1)S(1)} %collective-permute-done.3), channel_id=1, source_target_pairs={{1023,0},{0,1},{1,2},{2,3},{3,4},{4,5},{5,6},{6,7},{7,8},{8,9},{9,... | collective-permute-start | bytes 1179656 | tf_op jit(solution)/shard_map/ppermute | solution.py:16
  77.7 14.5 %collective-permute-start.8 = (bf16[256,768]{1,0:T(8,128)(2,1)S(1)}, bf16[256,768]{1,0:T(8,128)(2,1)S(1)}, u32[]{:S(2)}, u32[]{:S(2)}) collective-permute-start(bf16[256,768]{1,0:T(8,128)(2,1)S(1)} %add_convert_fusion.1), channel_id=1, source_target_pairs={{1023,0},{0,1},{1,2},{2,3},{3,4},{4,5},{5,6},{6,7},{7,8},{8,9},{9,... | collective-permute-start | bytes 1179656 | tf_op jit(solution)/shard_map/ppermute | solution.py:16
  93.1 387.4 %collective-permute-start.9 = (bf16[256,768]{1,0:T(8,128)(2,1)}, bf16[256,768]{1,0:T(8,128)(2,1)}, u32[]{:S(2)}, u32[]{:S(2)}) collective-permute-start(bf16[256,768]{1,0:T(8,128)(2,1)} %add_convert_fusion), channel_id=1, source_target_pairs={{2,0},{3,1},{4,2},{5,3},{6,4},{7,5},{8,6},{9,7},{10,8},{11,9},{12,... | collective-permute-start | bytes 1179656 | tf_op jit(solution)/shard_map/ppermute | solution.py:16
  105.7 1.0 copy-start.2
  106.0 0.7 copy-start.1
  321.8 2.3 copy-start.4
Sparse Core Ops, SparseCore 0:
  321.9 157.1 reduce-scatter.2
where the time goes:
time: 491 us; the launch traced here: 489 us
  blocking collectives  213 us (43%)
  waiting for transfers between devices  186 us (38%)
  starting transfers between devices  55.8 us (11%)
  between operations  15.1 us (3%)
  matrix products  11 us (2%)
  local copies, waits for them, and re-layouts  5.25 us (1%)
    unnamed x1, blocking collectives  213 us
    reduce_scatter x1, waiting for transfers between devices, local(): lax.psum_scatter(partial_rows.astype(jnp.bfloat16), 'col', scatter_dimens...  155 us
    ppermute x10, starting transfers between devices, passed_along(): return lax.ppermute(block, axis, route)  55.8 us
    ppermute x10, waiting for transfers between devices, passed_along(): return lax.ppermute(block, axis, route)  31.1 us
  transfers between devices with their start and end apart: 11, of which 9 were waited for; matrix products, arithmetic and copies ran while one was open for 3% of the time, Pallas kernels for 0%

commit v1 on v0

v1 whole, which is shorter than its diff:
```python
import jax
import jax.numpy as jnp
from jax import lax
from jax.sharding import PartitionSpec as P

HALF = 2
TEMP = 10.0
BIAS = -4.0
LOOP = ("row", "col")
BF16 = jnp.bfloat16
F32 = jnp.float32


def from_ahead(block, distance):
    n = lax.axis_size(LOOP)
    return lax.ppermute(block, LOOP, [((i + distance) % n, i) for i in range(n)])


def dot(a, b, dims):
    return lax.dot_general(a, b, (dims, ((), ())), preferred_element_type=F32)


def loss_and_slope(logit, match):
    label = jnp.where(match, 1.0, -1.0).astype(F32)
    z = -label * logit
    return jax.nn.softplus(z), (-label * jax.nn.sigmoid(z)).astype(BF16)


def local(image_feats, text_emb, head_weight, partner):
    rows, width = image_feats.shape
    blocks = lax.axis_size(LOOP)
    here = lax.axis_index(LOOP)
    offsets = [o for o in range(-HALF, HALF + 1) if o]

    texts = {o: from_ahead(text_emb, o) for o in sorted(offsets, key=abs, reverse=True)}
    texts[0] = text_emb

    proj = dot(image_feats, head_weight, ((1,), (0,)))
    norm = jnp.sqrt(jnp.sum(proj * proj, axis=1, keepdims=True) + 1e-06)
    unit = proj / norm
    unit_b = unit.astype(BF16)

    place = (partner // rows - here + HALF) % blocks
    within = partner % rows
    codes = jnp.stack([place, within]).astype(BF16)
    parcel = jnp.concatenate([unit_b, jnp.pad(codes, ((0, 14), (0, width - rows)))])
    parcels = {o: from_ahead(parcel, o) for o in sorted(offsets, key=abs, reverse=True)}
    parcels[0] = parcel

    row_loss = jnp.zeros((rows,), F32)
    unit_grad = jnp.zeros(proj.shape, F32)
    column = lax.broadcasted_iota(jnp.int32, (rows, rows), 1)
    for o in (0, -2, 2, -1, 1):
        logit = TEMP * dot(unit_b, texts[o], ((1,), (1,))) + BIAS
        match = (place[:, None] == o + HALF) & (within[:, None] == column)
        loss, slope = loss_and_slope(logit, match)
        row_loss = row_loss + jnp.sum(loss, axis=1)
        unit_grad = unit_grad + TEMP * dot(slope, texts[o], ((1,), (0,)))
    inner = jnp.sum(unit * unit_grad, axis=1, keepdims=True)
    proj_grad = ((unit_grad - unit * inner) / norm).astype(BF16)

    n_col, n_row = lax.axis_size("col"), lax.axis_size("row")
    cols, tall = width // n_col, width // n_row
    terms = dot(proj_grad, image_feats, ((0,), (0,))).astype(BF16)
    mine = lax.all_to_all(terms.reshape(n_col, cols, width), "col", 0, 0, tiled=True)
    pick = jnp.tile(jnp.eye(cols, dtype=BF16), (n_col, 1))
    summed = dot(mine.reshape(width, width), pick, ((0,), (0,))).astype(BF16)
    last = lax.all_to_all(summed.reshape(n_row, 8, tall * cols // 8), "row", 0, 0, tiled=True)
    head_grad = jnp.sum(last.astype(F32), axis=0).reshape(tall, cols)

    feat_grad = dot(proj_grad, head_weight, ((1,), (1,))).astype(BF16)

    text_grad = jnp.zeros(proj.shape, F32)
    line = lax.broadcasted_iota(F32, (rows, rows), 0)
    for o in (0, -2, 2, -1, 1):
        units = parcels[o][:rows]
        info = parcels[o][rows:].astype(F32)
        logit = TEMP * dot(text_emb, units, ((1,), (1,))) + BIAS
        match = (info[0:1, :rows] == HALF - o) & (info[1:2, :rows] == line)
        _, slope = loss_and_slope(logit, match)
        text_grad = text_grad + TEMP * dot(slope, units, ((1,), (0,)))
    return row_loss, feat_grad, text_grad, head_grad


def solution(mesh):
    split = P(LOOP)
    return jax.shard_map(
        local,
        mesh=mesh,
        in_specs=(P(LOOP, None), P(LOOP, None), P(), split),
        out_specs=(split, P(LOOP, None), P(LOOP, None), P("row", "col")),
        check_vma=False,
    )
```

time: 491 us -> 165 us (0.34)
  blocking collectives: 213 us -> 0 us
  waiting for transfers between devices: 186 us -> 62.3 us
  between operations: 15.1 us -> 0.94 us
  starting transfers between devices: 55.8 us -> 68.6 us
  matrix products: 11 us -> 22.2 us
    unnamed x1 -> x0, blocking collectives: 213 us -> none
    reduce_scatter x1 -> x0, waiting for transfers between devices: 155 us -> none  [local(): lax.psum_scatter(partial_rows.astype(jnp.bfloat16), 'col', scatter_dimens...]
    all_to_all x0 -> x2, waiting for transfers between devices: none -> 31.1 us  [the longest x1 22.4 us: local(): lax.all_to_all(summed.reshape(n_row, 8, tall * cols // 8), 'row', 0, 0, t...]
    all_to_all x0 -> x2, starting transfers between devices: none -> 21.3 us  [the longest x1 16.2 us: local(): lax.all_to_all(summed.reshape(n_row, 8, tall * cols // 8), 'row', 0, 0, t...]
    dot_general x18 -> x19, matrix products: 11 us -> 22.2 us  [dot(): return lax.dot_general(a, b, (dims, ((), ())), preferred_element_type=F32)]
    ppermute x10 -> x8, starting transfers between devices: 55.8 us -> 47.3 us  [from_ahead(): lax.ppermute(block, LOOP, [((i + distance) % n, i) for i in range(n)])]
    ppermute x10 -> x8, waiting for transfers between devices: 31.1 us -> 31.2 us  [from_ahead(): lax.ppermute(block, LOOP, [((i + distance) % n, i) for i in range(n)])]
  transfers between devices with their start and end apart: 11 -> 10, of which waited for: 9 -> 6; matrix products, arithmetic and copies ran while one was open for 3% -> 14% of each run, Pallas kernels for 0% -> 0%
where the time goes in v1:
time: 165 us; the launch traced here: 162 us
  starting transfers between devices  68.6 us (42%)
  waiting for transfers between devices  62.3 us (38%)
  matrix products  22.2 us (13%)
  other arithmetic  4.13 us (3%)
  local copies, waits for them, and re-layouts  3.77 us (2%)
    ppermute x8, starting transfers between devices, from_ahead(): lax.ppermute(block, LOOP, [((i + distance) % n, i) for i in range(n)])  47.3 us
    ppermute x8, waiting for transfers between devices, from_ahead(): lax.ppermute(block, LOOP, [((i + distance) % n, i) for i in range(n)])  31.2 us
    all_to_all x1, waiting for transfers between devices, local(): lax.all_to_all(summed.reshape(n_row, 8, tall * cols // 8), 'row', 0, 0, t...  22.4 us
    dot_general x19, matrix products, dot(): return lax.dot_general(a, b, (dims, ((), ())), preferred_element_type=F32)  22.2 us
    all_to_all x1, starting transfers between devices, local(): lax.all_to_all(summed.reshape(n_row, 8, tall * cols // 8), 'row', 0, 0, t...  16.2 us
    all_to_all x1, waiting for transfers between devices, local(): lax.all_to_all(terms.reshape(n_col, cols, width), 'col', 0, 0, tiled=True)  8.69 us
    all_to_all x1, starting transfers between devices, local(): lax.all_to_all(terms.reshape(n_col, cols, width), 'col', 0, 0, tiled=True)  5.08 us
  transfers between devices with their start and end apart: 10, of which 6 were waited for; matrix products, arithmetic and copies ran while one was open for 14% of the time, Pallas kernels for 0%

profile of v1, /device:TPU:1, one launch (start us, length us, event | category | flops | bytes accessed | tf_op | source)
XLA Modules:
  0.0 161.9 jit_solution(15876312379333311243)
XLA Ops:
  0.7 1.3 copy-done
  1.9 1.6 multiply_reduce_fusion.1
  3.6 0.1 fusion.187
  3.7 0.8 pad_maximum_fusion
  4.5 4.0 %collective-permute-start.4 = (bf16[272,768]{1,0:T(8,128)(2,1)}, bf16[272,768]{1,0:T(8,128)(2,1)}, u32[]{:S(2)}, u32[]{:S(2)}) collective-permute-start(bf16[272,768]{1,0:T(8,128)(2,1)} %pad_maximum_fusion), channel_id=1, source_target_pairs={{1022,0},{1023,1},{0,2},{1,3},{2,4},{3,5},{4,6},{5,7},{6,8},{7,9},... | collective-permute-start | bytes 1253384 | tf_op jit(solution)/shard_map/ppermute | solution.py:16
  8.5 14.0 %collective-permute-start.7 = (bf16[272,768]{1,0:T(8,128)(2,1)}, bf16[272,768]{1,0:T(8,128)(2,1)}, u32[]{:S(2)}, u32[]{:S(2)}) collective-permute-start(bf16[272,768]{1,0:T(8,128)(2,1)} %pad_maximum_fusion), channel_id=1, source_target_pairs={{1,0},{2,1},{3,2},{4,3},{5,4},{6,5},{7,6},{8,7},{9,8},{10,9},{11,1... | collective-permute-start | bytes 1253384 | tf_op jit(solution)/shard_map/ppermute | solution.py:16
  22.5 1.9 %collective-permute-start.6 = (bf16[272,768]{1,0:T(8,128)(2,1)}, bf16[272,768]{1,0:T(8,128)(2,1)}, u32[]{:S(2)}, u32[]{:S(2)}) collective-permute-start(bf16[272,768]{1,0:T(8,128)(2,1)} %pad_maximum_fusion), channel_id=1, source_target_pairs={{1023,0},{0,1},{1,2},{2,3},{3,4},{4,5},{5,6},{6,7},{7,8},{8,9},{9,... | collective-permute-start | bytes 1253384 | tf_op jit(solution)/shard_map/ppermute | solution.py:16
  24.4 16.9 %collective-permute-start.5 = (bf16[272,768]{1,0:T(8,128)(2,1)}, bf16[272,768]{1,0:T(8,128)(2,1)S(1)}, u32[]{:S(2)}, u32[]{:S(2)}) collective-permute-start(bf16[272,768]{1,0:T(8,128)(2,1)} %pad_maximum_fusion), channel_id=1, source_target_pairs={{2,0},{3,1},{4,2},{5,3},{6,4},{7,5},{8,6},{9,7},{10,8},{11,9},{12,... | collective-permute-start | bytes 1253384 | tf_op jit(solution)/shard_map/ppermute | solution.py:16
  41.3 1.9 %collective-permute-start.2 = (bf16[256,768]{1,0:T(8,128)(2,1)S(1)}, bf16[256,768]{1,0:T(8,128)(2,1)S(1)}, u32[]{:S(2)}, u32[]{:S(2)}) collective-permute-start(bf16[256,768]{1,0:T(8,128)(2,1)S(1)} %copy-done.4), channel_id=1, source_target_pairs={{1023,0},{0,1},{1,2},{2,3},{3,4},{4,5},{5,6},{6,7},{7,8},{8,9},{9,... | collective-permute-start | bytes 1179656 | tf_op jit(solution)/shard_map/ppermute | solution.py:16
  43.3 0.5 fusion.62
  43.8 0.4 fusion.96
  44.2 1.3 fusion.97
  45.5 2.4 %collective-permute-done.2 = bf16[256,768]{1,0:T(8,128)(2,1)S(1)} collective-permute-done((bf16[256,768]{1,0:T(8,128)(2,1)S(1)}, bf16[256,768]{1,0:T(8,128)(2,1)S(1)}, u32[]{:S(2)}, u32[]{:S(2)}) %collective-permute-start.2) | collective-permute-done | bytes 393248 | tf_op jit(solution)/shard_map/ppermute | solution.py:16
  47.9 4.8 %collective-permute-start.3 = (bf16[256,768]{1,0:T(8,128)(2,1)S(1)}, bf16[256,768]{1,0:T(8,128)(2,1)S(1)}, u32[]{:S(2)}, u32[]{:S(2)}) collective-permute-start(bf16[256,768]{1,0:T(8,128)(2,1)S(1)} %copy-done.4), channel_id=1, source_target_pairs={{1,0},{2,1},{3,2},{4,3},{5,4},{6,5},{7,6},{8,7},{9,8},{10,9},{11,1... | collective-permute-start | bytes 1179656 | tf_op jit(solution)/shard_map/ppermute | solution.py:16
  52.7 0.5 fusion.65
  53.2 0.4 fusion.99
  53.6 4.2 %collective-permute-done.3 = bf16[256,768]{1,0:T(8,128)(2,1)S(1)} collective-permute-done((bf16[256,768]{1,0:T(8,128)(2,1)S(1)}, bf16[256,768]{1,0:T(8,128)(2,1)S(1)}, u32[]{:S(2)}, u32[]{:S(2)}) %collective-permute-start.3) | collective-permute-done | bytes 393248 | tf_op jit(solution)/shard_map/ppermute | solution.py:16
  57.8 1.9 %collective-permute-start = (bf16[256,768]{1,0:T(8,128)(2,1)S(1)}, bf16[256,768]{1,0:T(8,128)(2,1)S(1)}, u32[]{:S(2)}, u32[]{:S(2)}) collective-permute-start(bf16[256,768]{1,0:T(8,128)(2,1)S(1)} %copy-done.4), channel_id=1, source_target_pairs={{1022,0},{1023,1},{0,2},{1,3},{2,4},{3,5},{4,6},{5,7},{6,8},{7,9},... | collective-permute-start | bytes 1179656 | tf_op jit(solution)/shard_map/ppermute | solution.py:16
  59.7 0.5 fusion.66
  60.2 0.4 fusion.100
  60.6 15.6 %collective-permute-done = bf16[256,768]{1,0:T(8,128)(2,1)S(1)} collective-permute-done((bf16[256,768]{1,0:T(8,128)(2,1)S(1)}, bf16[256,768]{1,0:T(8,128)(2,1)S(1)}, u32[]{:S(2)}, u32[]{:S(2)}) %collective-permute-start) | collective-permute-done | bytes 393248 | tf_op jit(solution)/shard_map/ppermute | solution.py:16
  76.2 1.9 %collective-permute-start.1 = (bf16[256,768]{1,0:T(8,128)(2,1)S(1)}, bf16[256,768]{1,0:T(8,128)(2,1)S(1)}, u32[]{:S(2)}, u32[]{:S(2)}) collective-permute-start(bf16[256,768]{1,0:T(8,128)(2,1)S(1)} %copy-done.4), channel_id=1, source_target_pairs={{2,0},{3,1},{4,2},{5,3},{6,4},{7,5},{8,6},{9,7},{10,8},{11,9},{12,... | collective-permute-start | bytes 1179656 | tf_op jit(solution)/shard_map/ppermute | solution.py:16
  78.1 0.5 fusion.63
  78.6 0.4 convolution_add_fusion.3
  79.0 9.0 %collective-permute-done.1 = bf16[256,768]{1,0:T(8,128)(2,1)S(1)} collective-permute-done((bf16[256,768]{1,0:T(8,128)(2,1)S(1)}, bf16[256,768]{1,0:T(8,128)(2,1)S(1)}, u32[]{:S(2)}, u32[]{:S(2)}) %collective-permute-start.1) | collective-permute-done | bytes 393248 | tf_op jit(solution)/shard_map/ppermute | solution.py:16
  88.0 0.5 fusion.64
  88.5 0.6 multiply_reduce_fusion
  89.1 0.2 divide_convert_fusion
  89.3 0.8 copy-done.1
  90.1 1.5 convolution_convert_fusion
  91.6 5.1 %all-to-all-start = ((bf16[16,48,768]{2,1,0:T(8,128)(2,1)}), bf16[16,48,768]{2,1,0:T(8,128)(2,1)S(1)}, u32[]{:S(2)}, u32[]{:S(2)}) async-start(bf16[16,48,768]{2,1,0:T(8,128)(2,1)} %bitcast.10), calls=%async_computation | async-start | bytes 2359296 | tf_op jit(solution)/shard_map/all_to_all | solution.py:65
  96.7 1.3 convolution_convert_fusion.1
  98.0 0.6 add_add_fusion
  98.5 0.7 slice_convert_fusion.3
  99.3 0.7 slice_convert_fusion
  100.0 0.7 slice_convert_fusion.1
  100.9 2.8 %fusion.51 = f32[256,768]{1,0:T(8,128)} fusion(bf16[256,768]{1,0:T(8,128)(2,1)} %param.5, bf16[272,768]{1,0:T(8,128)(2,1)} %collective-permute-done.7, f32[256]{0:T(256)S(1)} %bitcast.127, pred[256]{0:T(512)(128)(4,1)S(1)} %compare_reduce_fusion), kind=kOutput, calls=%fused_computation.67 | convolution fusion | flops 202113024 | bytes 1967360 | tf_op jit(solution)/shard_map/dot_general | solution.py:20
  103.8 3.0 %convolution_add_fusion.1 = f32[256,768]{1,0:T(8,128)} fusion(f32[256,768]{1,0:T(8,128)} %fusion.97, bf16[256,768]{1,0:T(8,128)(2,1)S(1)} %copy-done.5, bf16[272,768]{1,0:T(8,128)(2,1)} %collective-permute-done.4, f32[256]{0:T(256)S(1)} %bitcast.126, pred[256]{0:T(512)(128)(4,1)S(1)} %compare_reduce_fusion.3), kind=kOutput, calls=%fused_computation.5 | convolution fusion | flops 202309632 | bytes 2753792 | tf_op jit(solution)/shard_map/dot_general | solution.py:20
  106.8 8.7 %all-to-all-done = bf16[16,48,768]{2,1,0:T(8,128)(2,1)S(1)} async-done(((bf16[16,48,768]{2,1,0:T(8,128)(2,1)}), bf16[16,48,768]{2,1,0:T(8,128)(2,1)S(1)}, u32[]{:S(2)}, u32[]{:S(2)}) %all-to-all-start) | async-done | bytes 1179680 | tf_op jit(solution)/shard_map/all_to_all | solution.py:65
  115.4 0.3 fusion.53
  115.8 0.2 copy.48
  116.0 0.8 reshape.48
  116.8 16.2 %all-to-all-start.1 = ((bf16[64,8,72]{2,1,0:T(8,128)(2,1)}), bf16[64,8,72]{2,1,0:T(8,128)(2,1)S(1)}, u32[]{:S(2)}, u32[]{:S(2)}) async-start(bf16[64,8,72]{2,1,0:T(8,128)(2,1)} %reshape.48), calls=%async_computation.1 | async-start | bytes 262144 | tf_op jit(solution)/shard_map/all_to_all | solution.py:68
  133.0 2.9 %fusion.52 = f32[256,768]{1,0:T(8,128)} fusion(bf16[256,768]{1,0:T(8,128)(2,1)} %param.5, bf16[272,768]{1,0:T(8,128)(2,1)} %collective-permute-done.6, f32[256]{0:T(256)S(1)} %bitcast.125, pred[256]{0:T(512)(128)(4,1)S(1)} %compare_reduce_fusion.1), kind=kOutput, calls=%fused_computation.68 | convolution fusion | flops 202113024 | bytes 1967360 | tf_op jit(solution)/shard_map/dot_general | solution.py:20
  135.9 2.8 %fusion.2 = f32[256,768]{1,0:T(8,128)} fusion(f32[256,768]{1,0:T(8,128)S(1)} %copy-done.2, f32[256,768]{1,0:T(8,128)} %fusion.52, f32[256,768]{1,0:T(8,128)S(1)} %copy-done.3, bf16[256,768]{1,0:T(8,128)(2,1)} %param.5, bf16[272,768]{1,0:T(8,128)(2,1)S(1)} %collective-permute-done.5, f32[256]{0:T(256)S(1)} %bitcast.124, ...), kind=kOutput, calls=%fused_computation.4 | convolution fusion | flops 202899456 | bytes 4326912 | tf_op jit(solution)/shard_map/dot_general | solution.py:20
  138.8 22.4 %all-to-all-done.1 = bf16[64,8,72]{2,1,0:T(8,128)(2,1)S(1)} async-done(((bf16[64,8,72]{2,1,0:T(8,128)(2,1)}), bf16[64,8,72]{2,1,0:T(8,128)(2,1)S(1)}, u32[]{:S(2)}, u32[]{:S(2)}) %all-to-all-start.1) | async-done | bytes 73760 | tf_op jit(solution)/shard_map/all_to_all | solution.py:68
  161.2 0.1 convert_reduce_fusion
  161.3 0.7 reshape.49
  (34 shorter events, 0.2 us)
Async XLA Ops:
  0.6 1.3 copy-start
  1.9 1.6 copy-start.6
  3.5 37.8 %copy-start.4 = (bf16[256,768]{1,0:T(8,128)(2,1)S(1)}, bf16[256,768]{1,0:T(8,128)(2,1)}, u32[]{:S(2)}) copy-start(bf16[256,768]{1,0:T(8,128)(2,1)} %param.5) | copy-start | bytes 1179652
  4.5 94.1 %collective-permute-start.4 = (bf16[272,768]{1,0:T(8,128)(2,1)}, bf16[272,768]{1,0:T(8,128)(2,1)}, u32[]{:S(2)}, u32[]{:S(2)}) collective-permute-start(bf16[272,768]{1,0:T(8,128)(2,1)} %pad_maximum_fusion), channel_id=1, source_target_pairs={{1022,0},{1023,1},{0,2},{1,3},{2,4},{3,5},{4,6},{5,7},{6,8},{7,9},... | collective-permute-start | bytes 1253384 | tf_op jit(solution)/shard_map/ppermute | solution.py:16
  8.5 90.8 %collective-permute-start.7 = (bf16[272,768]{1,0:T(8,128)(2,1)}, bf16[272,768]{1,0:T(8,128)(2,1)}, u32[]{:S(2)}, u32[]{:S(2)}) collective-permute-start(bf16[272,768]{1,0:T(8,128)(2,1)} %pad_maximum_fusion), channel_id=1, source_target_pairs={{1,0},{2,1},{3,2},{4,3},{5,4},{6,5},{7,6},{8,7},{9,8},{10,9},{11,1... | collective-permute-start | bytes 1253384 | tf_op jit(solution)/shard_map/ppermute | solution.py:16
  22.5 77.6 %collective-permute-start.6 = (bf16[272,768]{1,0:T(8,128)(2,1)}, bf16[272,768]{1,0:T(8,128)(2,1)}, u32[]{:S(2)}, u32[]{:S(2)}) collective-permute-start(bf16[272,768]{1,0:T(8,128)(2,1)} %pad_maximum_fusion), channel_id=1, source_target_pairs={{1023,0},{0,1},{1,2},{2,3},{3,4},{4,5},{5,6},{6,7},{7,8},{8,9},{9,... | collective-permute-start | bytes 1253384 | tf_op jit(solution)/shard_map/ppermute | solution.py:16
  24.4 76.4 %collective-permute-start.5 = (bf16[272,768]{1,0:T(8,128)(2,1)}, bf16[272,768]{1,0:T(8,128)(2,1)S(1)}, u32[]{:S(2)}, u32[]{:S(2)}) collective-permute-start(bf16[272,768]{1,0:T(8,128)(2,1)} %pad_maximum_fusion), channel_id=1, source_target_pairs={{2,0},{3,1},{4,2},{5,3},{6,4},{7,5},{8,6},{9,7},{10,8},{11,9},{12,... | collective-permute-start | bytes 1253384 | tf_op jit(solution)/shard_map/ppermute | solution.py:16
  41.3 6.6 %collective-permute-start.2 = (bf16[256,768]{1,0:T(8,128)(2,1)S(1)}, bf16[256,768]{1,0:T(8,128)(2,1)S(1)}, u32[]{:S(2)}, u32[]{:S(2)}) collective-permute-start(bf16[256,768]{1,0:T(8,128)(2,1)S(1)} %copy-done.4), channel_id=1, source_target_pairs={{1023,0},{0,1},{1,2},{2,3},{3,4},{4,5},{5,6},{6,7},{7,8},{8,9},{9,... | collective-permute-start | bytes 1179656 | tf_op jit(solution)/shard_map/ppermute | solution.py:16
  47.9 9.8 %collective-permute-start.3 = (bf16[256,768]{1,0:T(8,128)(2,1)S(1)}, bf16[256,768]{1,0:T(8,128)(2,1)S(1)}, u32[]{:S(2)}, u32[]{:S(2)}) collective-permute-start(bf16[256,768]{1,0:T(8,128)(2,1)S(1)} %copy-done.4), channel_id=1, source_target_pairs={{1,0},{2,1},{3,2},{4,3},{5,4},{6,5},{7,6},{8,7},{9,8},{10,9},{11,1... | collective-permute-start | bytes 1179656 | tf_op jit(solution)/shard_map/ppermute | solution.py:16
  57.8 18.4 %collective-permute-start = (bf16[256,768]{1,0:T(8,128)(2,1)S(1)}, bf16[256,768]{1,0:T(8,128)(2,1)S(1)}, u32[]{:S(2)}, u32[]{:S(2)}) collective-permute-start(bf16[256,768]{1,0:T(8,128)(2,1)S(1)} %copy-done.4), channel_id=1, source_target_pairs={{1022,0},{1023,1},{0,2},{1,3},{2,4},{3,5},{4,6},{5,7},{6,8},{7,9},... | collective-permute-start | bytes 1179656 | tf_op jit(solution)/shard_map/ppermute | solution.py:16
  76.2 11.8 %collective-permute-start.1 = (bf16[256,768]{1,0:T(8,128)(2,1)S(1)}, bf16[256,768]{1,0:T(8,128)(2,1)S(1)}, u32[]{:S(2)}, u32[]{:S(2)}) collective-permute-start(bf16[256,768]{1,0:T(8,128)(2,1)S(1)} %copy-done.4), channel_id=1, source_target_pairs={{2,0},{3,1},{4,2},{5,3},{6,4},{7,5},{8,6},{9,7},{10,8},{11,9},{12,... | collective-permute-start | bytes 1179656 | tf_op jit(solution)/shard_map/ppermute | solution.py:16
  89.1 1.0 copy-start.1
  91.6 23.8 %all-to-all-start = ((bf16[16,48,768]{2,1,0:T(8,128)(2,1)}), bf16[16,48,768]{2,1,0:T(8,128)(2,1)S(1)}, u32[]{:S(2)}, u32[]{:S(2)}) async-start(bf16[16,48,768]{2,1,0:T(8,128)(2,1)} %bitcast.10), calls=%async_computation | async-start | bytes 2359296 | tf_op jit(solution)/shard_map/all_to_all | solution.py:65
  100.9 2.9 %copy-start.5 = (bf16[256,768]{1,0:T(8,128)(2,1)S(1)}, bf16[256,768]{1,0:T(8,128)(2,1)}, u32[]{:S(2)}) copy-start(bf16[256,768]{1,0:T(8,128)(2,1)} %param.5) | copy-start | bytes 1179652
  116.8 44.4 %all-to-all-start.1 = ((bf16[64,8,72]{2,1,0:T(8,128)(2,1)}), bf16[64,8,72]{2,1,0:T(8,128)(2,1)S(1)}, u32[]{:S(2)}, u32[]{:S(2)}) async-start(bf16[64,8,72]{2,1,0:T(8,128)(2,1)} %reshape.48), calls=%async_computation.1 | async-start | bytes 262144 | tf_op jit(solution)/shard_map/all_to_all | solution.py:68
  133.0 2.9 %copy-start.2 = (f32[256,768]{1,0:T(8,128)S(1)}, f32[256,768]{1,0:T(8,128)}, u32[]{:S(2)}) copy-start(f32[256,768]{1,0:T(8,128)} %fusion.51) | copy-start | bytes 2359300
  133.0 2.9 %copy-start.3 = (f32[256,768]{1,0:T(8,128)S(1)}, f32[256,768]{1,0:T(8,128)}, u32[]{:S(2)}) copy-start(f32[256,768]{1,0:T(8,128)} %convolution_add_fusion.1) | copy-start | bytes 2359300

commit v2 on v1

v2 whole, which is shorter than its diff:
```python
import jax
import jax.numpy as jnp
from jax import lax
from jax.experimental import pallas as pl
from jax.experimental.pallas import tpu as pltpu
from jax.sharding import Mesh, PartitionSpec as P

HALF = 2
TEMP = 10.0
BIAS = -4.0
CORES = 2
TAIL = 16
ROW, CHIP, CORE = "row", "chip", "core"
LOOP = (ROW, CHIP, CORE)
COL = (CHIP, CORE)
BF16 = jnp.bfloat16
F32 = jnp.float32
VMEM = pl.BlockSpec(memory_space=pltpu.VMEM)
SMEM = pl.BlockSpec(memory_space=pltpu.SMEM)


def from_ahead(block, distance):
    n = lax.axis_size(LOOP)
    return lax.ppermute(block, LOOP, [((i + distance) % n, i) for i in range(n)])


def other_core(block):
    return lax.ppermute(block, CORE, [(0, 1), (1, 0)])


def after(value, *earlier):
    return lax.optimization_barrier((value, *earlier))[0]


def dot(a, b, dims):
    return lax.dot_general(a, b, (dims, ((), ())), preferred_element_type=F32)


def kernel_call(body, outs, args, flops, scalars=0):
    moved = sum(a.size * a.dtype.itemsize for a in args)
    moved += sum(o.size * o.dtype.itemsize for o in outs)
    return pl.pallas_call(
        body,
        out_shape=outs,
        in_specs=[SMEM] * scalars + [VMEM] * (len(args) - scalars),
        out_specs=[VMEM] * len(outs),
        compiler_params=pltpu.CompilerParams(vmem_limit_bytes=32 * 2**20),
        cost_estimate=pl.CostEstimate(flops=flops, bytes_accessed=moved, transcendentals=0),
    )(*args)


def prepare(blocks, here_ref, feats_ref, weight_ref, partner_ref, proj_ref, parcel_ref):
    rows, width = feats_ref.shape
    proj = jnp.dot(feats_ref[...], weight_ref[...], preferred_element_type=F32)
    proj_ref[...] = proj
    norm = jnp.sqrt(jnp.sum(proj * proj, axis=1, keepdims=True) + 1e-06)
    parcel_ref[:rows, :] = (proj / norm).astype(BF16)
    partner = partner_ref[...]
    block = lax.div(partner, rows)
    place = block - here_ref[0] + HALF
    place = jnp.where(place < 0, place + blocks, place)
    place = jnp.where(place >= blocks, place - blocks, place)
    line = lax.broadcasted_iota(jnp.int32, (TAIL, rows), 0)
    codes = jnp.where(line == 0, place, jnp.where(line == 1, partner - block * rows, 0))
    parcel_ref[rows:, :] = jnp.zeros((TAIL, width), BF16)
    parcel_ref[rows:, :rows] = codes.astype(F32).astype(BF16)


def pair_terms(text, parcel_ref, place, with_loss=True):
    rows = text.shape[0]
    codes = parcel_ref[rows:, :rows].astype(F32)
    target = (codes[0:1] - (place + HALF)) * rows + codes[1:2]
    match = lax.broadcasted_iota(jnp.int32, (rows, rows), 0).astype(F32) == target
    logit = TEMP * dot(text, parcel_ref[:rows, :], ((1,), (1,))) + BIAS
    z = jnp.where(match, -logit, logit)
    small = jnp.exp(-jnp.abs(z))
    share = 1.0 / (1.0 + small)
    sigmoid = jnp.where(z >= 0, share, small * share)
    slope = jnp.where(match, -sigmoid, sigmoid).astype(BF16)
    if not with_loss:
        return slope
    loss = jnp.sum(jnp.maximum(z, 0.0) + jnp.log1p(small), axis=0, keepdims=True)
    return slope, loss


def image_start(side_ref, parcel_ref, own_ref, mate_ref, ahead_ref, behind_ref, grad_ref, loss_ref):
    side = side_ref[0].astype(F32)
    grad, total = None, None
    for text_ref, place in ((own_ref, 0), (mate_ref, side), (ahead_ref, HALF), (behind_ref, -HALF)):
        text = text_ref[...]
        slope, loss = pair_terms(text, parcel_ref, place)
        part = dot(slope, text, ((0,), (0,)))
        grad, total = (part, loss) if grad is None else (grad + part, total + loss)
    grad_ref[...] = grad
    loss_ref[...] = total


def image_end(
    side_ref, parcel_ref, far_ref, proj_ref, grad_ref, loss_ref, feats_ref, back_ref, terms_ref, out_loss_ref
):
    half = feats_ref.shape[1] // 2
    far = far_ref[...]
    slope, loss = pair_terms(far, parcel_ref, -side_ref[0].astype(F32))
    out_loss_ref[...] = loss_ref[...] + loss
    unit_grad = TEMP * (grad_ref[...] + dot(slope, far, ((0,), (0,))))
    proj = proj_ref[...]
    norm = jnp.sqrt(jnp.sum(proj * proj, axis=1, keepdims=True) + 1e-06)
    unit = proj / norm
    inner = jnp.sum(unit * unit_grad, axis=1, keepdims=True)
    back = ((unit_grad - unit * inner) / norm).astype(BF16)
    back_ref[...] = back
    terms_ref[:, :half] = dot(back, feats_ref[:, half:], ((0,), (0,))).astype(BF16)
    terms_ref[:, half:] = dot(back, feats_ref[:, :half], ((0,), (0,))).astype(BF16)


def text_side(side_ref, text_ref, own_ref, mate_ref, ahead_ref, behind_ref, far_ref, grad_ref):
    rows = text_ref.shape[0]
    side = side_ref[0].astype(F32)
    text = text_ref[...]
    grad = None
    for parcel_ref, place in ((own_ref, 0), (mate_ref, -side), (ahead_ref, -HALF), (behind_ref, HALF), (far_ref, side)):
        slope = pair_terms(text, parcel_ref, place, with_loss=False)
        part = dot(slope, parcel_ref[:rows, :], ((1,), (0,)))
        grad = part if grad is None else grad + part
    grad_ref[...] = TEMP * grad


def local(image_feats, text_emb, head_weight, partner):
    rows, width = image_feats.shape
    blocks = lax.axis_size(LOOP)
    core = lax.axis_index(CORE)
    here = lax.axis_index(LOOP).astype(jnp.int32).reshape(1)
    side = (1 - 2 * core).astype(jnp.int32).reshape(1)
    shape = jax.ShapeDtypeStruct
    product = 2 * rows * width * width
    pair = 2 * rows * rows * width

    ahead, behind = from_ahead(text_emb, HALF), from_ahead(text_emb, -HALF)
    mate = other_core(text_emb)

    proj, parcel = kernel_call(
        lambda *refs: prepare(blocks, *refs),
        [shape((rows, width), F32), shape((rows + TAIL, width), BF16)],
        [here, image_feats, head_weight, partner.reshape(1, rows)],
        product,
        1,
    )
    ahead, behind, parcel = lax.optimization_barrier((ahead, behind, parcel))
    far = other_core(jnp.where(core == 0, ahead, behind))
    grad, loss = kernel_call(
        image_start,
        [shape((rows, width), F32), shape((1, rows), F32)],
        [side, parcel, text_emb, mate, ahead, behind],
        8 * pair,
        1,
    )
    proj_grad, terms, row_loss = kernel_call(
        image_end,
        [shape((rows, width), BF16), shape((width, width), BF16), shape((1, rows), F32)],
        [side, parcel, far, proj, grad, loss, image_feats],
        2 * pair + product,
        1,
    )
    sent = after(parcel, terms)
    parcel_ahead, parcel_behind = from_ahead(sent, HALF), from_ahead(sent, -HALF)
    parcel_mate = other_core(sent)
    parcel_far = other_core(jnp.where(core == 0, parcel_ahead, parcel_behind))

    n_col, n_row = lax.axis_size(COL), lax.axis_size(ROW)
    cols, tall = width // n_col, width // n_row
    mine = lax.all_to_all(terms.reshape(n_col, cols, width), COL, 0, 0, tiled=True)

    (text_grad,) = kernel_call(
        text_side,
        [shape((rows, width), F32)],
        [side, text_emb, parcel, parcel_mate, parcel_ahead, parcel_behind, parcel_far],
        10 * pair,
        1,
    )
    feat_grad = dot(proj_grad, head_weight, ((1,), (1,))).astype(BF16)

    pick = jnp.tile(jnp.eye(cols, dtype=BF16), (n_col, 1))
    summed = dot(mine.reshape(width, width), pick, ((0,), (0,))).astype(BF16)
    order = [(i + n_row // 2) % n_row for i in range(n_row)]
    last = lax.all_to_all(
        summed.reshape(n_row, 8, tall * cols // 8), ROW, 0, 0, axis_index_groups=[order], tiled=True
    )
    head_grad = jnp.sum(last.astype(F32), axis=0).reshape(tall, cols)
    return row_loss.reshape(rows), feat_grad, text_grad, head_grad


def solution(mesh):
    n_row, n_col = mesh.devices.shape
    fine = Mesh(mesh.devices.reshape(n_row, n_col // CORES, CORES), LOOP)
    split = P(LOOP)
    return jax.shard_map(
        local,
        mesh=fine,
        in_specs=(P(LOOP, None), P(LOOP, None), P(), split),
        out_specs=(split, P(LOOP, None), P(LOOP, None), P(ROW, COL)),
        check_vma=False,
    )
```

time: 165 us -> 114 us (0.69); the launches traced: 162 us -> 113 us
  waiting for transfers between devices: 62.3 us -> 14.3 us
  matrix products: 22.2 us -> 1.6 us
  starting transfers between devices: 68.6 us -> 82.1 us
  Pallas kernels: 0 us -> 8.79 us
  other arithmetic: 4.13 us -> 0.92 us
    ppermute x8 -> x4, waiting for transfers between devices: 31.2 us -> 1.65 us  [from_ahead(): lax.ppermute(block, LOOP, [((i + distance) % n, i) for i in range(n)])]
    dot_general x19 -> x2, matrix products: 22.2 us -> 1.6 us  [dot(): return lax.dot_general(a, b, (dims, ((), ())), preferred_element_type=F32)]
    all_to_all x2, waiting for transfers between devices: 31.1 us -> 12.5 us  [the longest x1 8.31 us: local(): lax.all_to_all(terms.reshape(n_col, cols, width), COL, 0, 0, tiled=True)]
    ppermute x0 -> x4, starting transfers between devices: none -> 12.6 us  [other_core(): return lax.ppermute(block, CORE, [(0, 1), (1, 0)])]
    pallas_call x0 -> x4, Pallas kernels: none -> 8.79 us  [kernel_call(): pl.pallas_call(body, out_shape=outs, in_specs=[SMEM] * scalars + [VMEM] *...]
    all_to_all x2, starting transfers between devices: 21.3 us -> 29.3 us  [the longest x1 25.7 us: local(): lax.all_to_all(summed.reshape(n_row, 8, tall * cols // 8), ROW, 0, 0, axi...]
    ppermute x8 -> x4, starting transfers between devices: 47.3 us -> 40.2 us  [from_ahead(): lax.ppermute(block, LOOP, [((i + distance) % n, i) for i in range(n)])]
    convert_element_type x7 -> x0, other arithmetic: 2.56 us -> none  [the longest x5 2.24 us: local(): info = parcels[o][rows:].astype(F32)]
  transfers between devices with their start and end apart: 10 -> 10, of which waited for: 6 -> 5; matrix products, arithmetic and copies ran while one was open for 14% -> 3% of each run, Pallas kernels for 0% -> 5%
where the time goes in v2:
time: 114 us; the launch traced here: 113 us
  starting transfers between devices  82.1 us (72%)
  waiting for transfers between devices  14.3 us (13%)
  Pallas kernels  8.79 us (8%)
  local copies, waits for them, and re-layouts  4.62 us (4%)
  matrix products  1.6 us (1%)
    ppermute x4, starting transfers between devices, from_ahead(): lax.ppermute(block, LOOP, [((i + distance) % n, i) for i in range(n)])  40.2 us
    all_to_all x1, starting transfers between devices, local(): lax.all_to_all(summed.reshape(n_row, 8, tall * cols // 8), ROW, 0, 0, axi...  25.7 us
    ppermute x4, starting transfers between devices, other_core(): return lax.ppermute(block, CORE, [(0, 1), (1, 0)])  12.6 us
    pallas_call x4, Pallas kernels, kernel_call(): pl.pallas_call(body, out_shape=outs, in_specs=[SMEM] * scalars + [VMEM] *...  8.79 us
    all_to_all x1, waiting for transfers between devices, local(): lax.all_to_all(terms.reshape(n_col, cols, width), COL, 0, 0, tiled=True)  8.31 us
    all_to_all x1, waiting for transfers between devices, local(): lax.all_to_all(summed.reshape(n_row, 8, tall * cols // 8), ROW, 0, 0, axi...  4.24 us
    all_to_all x1, starting transfers between devices, local(): lax.all_to_all(terms.reshape(n_col, cols, width), COL, 0, 0, tiled=True)  3.6 us
    unnamed x14, local copies, waits for them, and re-layouts  2.96 us
  transfers between devices with their start and end apart: 10, of which 5 were waited for; matrix products, arithmetic and copies ran while one was open for 3% of the time, Pallas kernels for 5%

profile of v2, /device:TPU:1, one launch (start us, length us, event | category | flops | bytes accessed | tf_op | source)
XLA Modules:
  0.0 113.2 jit_solution(11766054569225350746)
XLA Ops:
  0.6 4.0 %collective-permute-start.1 = (bf16[256,768]{1,0:T(8,128)(2,1)}, bf16[256,768]{1,0:T(8,128)(2,1)S(1)}, u32[]{:S(2)}, u32[]{:S(2)}) collective-permute-start(bf16[256,768]{1,0:T(8,128)(2,1)} %text_ref.1), channel_id=1, source_target_pairs={{1022,0},{1023,1},{0,2},{1,3},{2,4},{3,5},{4,6},{5,7},{6,8},{7,9},... | collective-permute-start | bytes 1179656 | tf_op jit(solution)/shard_map/ppermute | solution.py:24
  4.7 21.8 %collective-permute-start = (bf16[256,768]{1,0:T(8,128)(2,1)}, bf16[256,768]{1,0:T(8,128)(2,1)S(1)}, u32[]{:S(2)}, u32[]{:S(2)}) collective-permute-start(bf16[256,768]{1,0:T(8,128)(2,1)} %text_ref.1), channel_id=1, source_target_pairs={{2,0},{3,1},{4,2},{5,3},{6,4},{7,5},{8,6},{9,7},{10,8},{11,9},{12,... | collective-permute-start | bytes 1179656 | tf_op jit(solution)/shard_map/ppermute | solution.py:24
  26.4 2.9 %collective-permute-start.3 = (bf16[256,768]{1,0:T(8,128)(2,1)}, bf16[256,768]{1,0:T(8,128)(2,1)S(1)}, u32[]{:S(2)}, u32[]{:S(2)}) collective-permute-start(bf16[256,768]{1,0:T(8,128)(2,1)} %text_ref.1), channel_id=1, source_target_pairs={{0,1},{1,0},{2,3},{3,2},{4,5},{5,4},{6,7},{7,6},{8,9},{9,8},{10,11... | collective-permute-start | bytes 1179656 | tf_op jit(solution)/shard_map/ppermute | solution.py:28
  29.3 0.0 copy-start
  29.3 1.3 %copy-done = bf16[768,768]{1,0:T(8,128)(2,1)S(1)} copy-done((bf16[768,768]{1,0:T(8,128)(2,1)S(1)}, bf16[768,768]{1,0:T(8,128)(2,1)}, u32[]{:S(2)}) %copy-start) | copy-done | bytes 1179672
  30.6 0.0 copy-start.2
  30.6 1.0 copy-done.2
  31.6 0.0 copy-start.4
  31.6 0.7 copy-done.4
  32.3 0.0 copy-start.5
  32.3 0.6 shard_map.75
  32.9 0.7 collective-permute-done.1.behind_ref
  33.5 1.0 collective-permute-done.ahead_ref
  34.5 0.8 broadcast_select_fusion.1
  35.3 3.4 %collective-permute-start.2 = (bf16[256,768]{1,0:T(8,128)(2,1)}, bf16[256,768]{1,0:T(8,128)(2,1)S(1)}, u32[]{:S(2)}, u32[]{:S(2)}) collective-permute-start(bf16[256,768]{1,0:T(8,128)(2,1)} %broadcast_select_fusion.1), channel_id=1, source_target_pairs={{0,1},{1,0},{2,3},{3,2},{4,5},{5,4},{6,7},{7,6},{8,9},{9,8},{10,11... | collective-permute-start | bytes 1179656 | tf_op jit(solution)/shard_map/ppermute | solution.py:28
  38.8 0.0 collective-permute-done.3.mate_ref
  38.8 0.0 copy-done.5
  38.8 0.0 copy-start.3
  38.8 2.4 %shard_map.76 = (f32[256,768]{1,0:T(8,128)S(1)}, f32[1,256]{1,0:T(1,128)S(1)}) custom-call(s32[1]{0:T(128)} %bitcast.side_ref, bf16[272,768]{1,0:T(8,128)(2,1)S(1)} %get-tuple-element.25.parcel_ref.own_ref, bf16[256,768]{1,0:T(8,128)(2,1)S(1)} %copy-done.5, bf16[256,768]{1,0:T(8,128)(2,1)S(1)} %collective-permute-done.3.mate_ref, ...), custom_call_target="tpu_custom_call" | custom-call | flops 805306368 | bytes 2778116 | tf_op jit(solution)/shard_map/pallas_call | solution.py:42
  41.2 0.0 collective-permute-done.2.far_ref
  41.2 0.0 copy-done.3
  41.3 2.7 %shard_map.77 = (bf16[256,768]{1,0:T(8,128)(2,1)S(1)}, bf16[768,768]{1,0:T(8,128)(2,1)}, f32[1,256]{1,0:T(1,128)}) custom-call(s32[1]{0:T(128)} %bitcast.side_ref, bf16[272,768]{1,0:T(8,128)(2,1)S(1)} %get-tuple-element.25.parcel_ref.own_ref, bf16[256,768]{1,0:T(8,128)(2,1)S(1)} %collective-permute-done.2.far_ref, ...), custom_call_target="tpu_custom_call" | custom-call | flops 503316480 | bytes 4352004 | tf_op jit(solution)/shard_map/pallas_call | solution.py:42
  44.0 3.6 %all-to-all-start = ((bf16[16,48,768]{2,1,0:T(8,128)(2,1)}), bf16[16,48,768]{2,1,0:T(8,128)(2,1)S(1)}, u32[]{:S(2)}, u32[]{:S(2)}) async-start(bf16[16,48,768]{2,1,0:T(8,128)(2,1)} %bitcast.4), calls=%async_computation | async-start | bytes 2359296 | tf_op jit(solution)/shard_map/all_to_all | solution.py:171
  47.6 3.2 %collective-permute-start.6 = (bf16[272,768]{1,0:T(8,128)(2,1)S(1)}, bf16[272,768]{1,0:T(8,128)(2,1)S(1)}, u32[]{:S(2)}, u32[]{:S(2)}) collective-permute-start(bf16[272,768]{1,0:T(8,128)(2,1)S(1)} %get-tuple-element.25.parcel_ref.own_ref), channel_id=1, source_target_pairs={{1022,0},{1023,1},{0,2},{1,3},{2,4},{3,5},{4,6},{5,7},{6,8},{7,9},... | collective-permute-start | bytes 1253384 | tf_op jit(solution)/shard_map/ppermute | solution.py:24
  50.8 11.2 %collective-permute-start.5 = (bf16[272,768]{1,0:T(8,128)(2,1)S(1)}, bf16[272,768]{1,0:T(8,128)(2,1)S(1)}, u32[]{:S(2)}, u32[]{:S(2)}) collective-permute-start(bf16[272,768]{1,0:T(8,128)(2,1)S(1)} %get-tuple-element.25.parcel_ref.own_ref), channel_id=1, source_target_pairs={{2,0},{3,1},{4,2},{5,3},{6,4},{7,5},{8,6},{9,7},{10,8},{11,9},{12,... | collective-permute-start | bytes 1253384 | tf_op jit(solution)/shard_map/ppermute | solution.py:24
  62.0 2.5 %collective-permute-start.4 = (bf16[272,768]{1,0:T(8,128)(2,1)S(1)}, bf16[272,768]{1,0:T(8,128)(2,1)S(1)}, u32[]{:S(2)}, u32[]{:S(2)}) collective-permute-start(bf16[272,768]{1,0:T(8,128)(2,1)S(1)} %get-tuple-element.25.parcel_ref.own_ref), channel_id=1, source_target_pairs={{0,1},{1,0},{2,3},{3,2},{4,5},{5,4},{6,7},{7,6},{8,9},{9,8},{10,11... | collective-permute-start | bytes 1253384 | tf_op jit(solution)/shard_map/ppermute | solution.py:28
  64.6 8.3 %all-to-all-done = bf16[16,48,768]{2,1,0:T(8,128)(2,1)S(1)} async-done(((bf16[16,48,768]{2,1,0:T(8,128)(2,1)}), bf16[16,48,768]{2,1,0:T(8,128)(2,1)S(1)}, u32[]{:S(2)}, u32[]{:S(2)}) %all-to-all-start) | async-done | bytes 1179680 | tf_op jit(solution)/shard_map/all_to_all | solution.py:171
  72.9 0.3 fusion
  73.3 0.0 copy-start.1
  73.3 0.2 copy.8
  73.4 0.8 reshape.46
  74.3 25.7 %all-to-all-start.1 = ((bf16[64,8,72]{2,1,0:T(8,128)(2,1)}), bf16[64,8,72]{2,1,0:T(8,128)(2,1)S(1)}, u32[]{:S(2)}, u32[]{:S(2)}) async-start(bf16[64,8,72]{2,1,0:T(8,128)(2,1)} %reshape.46), calls=%async_computation.1 | async-start | bytes 262144 | tf_op jit(solution)/shard_map/all_to_all | solution.py:185
  100.0 0.0 collective-permute-done.6.behind_ref
  100.0 0.0 collective-permute-done.5.ahead_ref
  100.0 0.1 broadcast_select_fusion
  100.1 0.0 copy-start.6
  100.1 3.8 %collective-permute-start.7 = (bf16[272,768]{1,0:T(8,128)(2,1)S(1)}, bf16[272,768]{1,0:T(8,128)(2,1)S(1)}, u32[]{:S(2)}, u32[]{:S(2)}) collective-permute-start(bf16[272,768]{1,0:T(8,128)(2,1)S(1)} %broadcast_select_fusion), channel_id=1, source_target_pairs={{0,1},{1,0},{2,3},{3,2},{4,5},{5,4},{6,7},{7,6},{8,9},{9,8},{10,11... | collective-permute-start | bytes 1253384 | tf_op jit(solution)/shard_map/ppermute | solution.py:28
  103.8 0.0 copy-done.1
  103.8 1.3 %convolution_convert_fusion = bf16[256,768]{1,0:T(8,128)(2,1)} fusion(bf16[256,768]{1,0:T(8,128)(2,1)S(1)} %get-tuple-element.23, bf16[768,768]{1,0:T(8,128)(2,1)S(1)} %copy-done.1), kind=kOutput, calls=%fused_computation | convolution fusion | flops 302186496 | bytes 1966080 | tf_op jit(solution)/shard_map/dot_general | solution.py:36
  105.1 0.0 collective-permute-done.4.mate_ref
  105.1 0.1 collective-permute-done.7.far_ref
  105.2 0.0 copy-done.6
  105.2 3.0 %shard_map.78 = f32[256,768]{1,0:T(8,128)} custom-call(s32[1]{0:T(128)} %bitcast.side_ref, bf16[256,768]{1,0:T(8,128)(2,1)S(1)} %copy-done.6, bf16[272,768]{1,0:T(8,128)(2,1)S(1)} %get-tuple-element.25.parcel_ref.own_ref, bf16[272,768]{1,0:T(8,128)(2,1)S(1)} %collective-permute-done.4.mate_ref, bf16[272,768]{1,0:T(8,128)(2,1)S(1)} %collective-permute-done.5.ahead_ref, ...), custom_call_target="tpu_custom_call" | custom-call | flops 1006632960 | bytes 3268612 | tf_op jit(solution)/shard_map/pallas_call | solution.py:42
  108.3 4.2 %all-to-all-done.1 = bf16[64,8,72]{2,1,0:T(8,128)(2,1)S(1)} async-done(((bf16[64,8,72]{2,1,0:T(8,128)(2,1)}), bf16[64,8,72]{2,1,0:T(8,128)(2,1)S(1)}, u32[]{:S(2)}, u32[]{:S(2)}) %all-to-all-start.1) | async-done | bytes 73760 | tf_op jit(solution)/shard_map/all_to_all | solution.py:185
  112.5 0.1 convert_reduce_fusion
  112.6 0.7 reshape.47
  (1 shorter events, 0.0 us)
Async XLA Ops:
  0.6 32.9 %collective-permute-start.1 = (bf16[256,768]{1,0:T(8,128)(2,1)}, bf16[256,768]{1,0:T(8,128)(2,1)S(1)}, u32[]{:S(2)}, u32[]{:S(2)}) collective-permute-start(bf16[256,768]{1,0:T(8,128)(2,1)} %text_ref.1), channel_id=1, source_target_pairs={{1022,0},{1023,1},{0,2},{1,3},{2,4},{3,5},{4,6},{5,7},{6,8},{7,9},... | collective-permute-start | bytes 1179656 | tf_op jit(solution)/shard_map/ppermute | solution.py:24
  4.7 29.8 %collective-permute-start = (bf16[256,768]{1,0:T(8,128)(2,1)}, bf16[256,768]{1,0:T(8,128)(2,1)S(1)}, u32[]{:S(2)}, u32[]{:S(2)}) collective-permute-start(bf16[256,768]{1,0:T(8,128)(2,1)} %text_ref.1), channel_id=1, source_target_pairs={{2,0},{3,1},{4,2},{5,3},{6,4},{7,5},{8,6},{9,7},{10,8},{11,9},{12,... | collective-permute-start | bytes 1179656 | tf_op jit(solution)/shard_map/ppermute | solution.py:24
  26.4 12.3 %collective-permute-start.3 = (bf16[256,768]{1,0:T(8,128)(2,1)}, bf16[256,768]{1,0:T(8,128)(2,1)S(1)}, u32[]{:S(2)}, u32[]{:S(2)}) collective-permute-start(bf16[256,768]{1,0:T(8,128)(2,1)} %text_ref.1), channel_id=1, source_target_pairs={{0,1},{1,0},{2,3},{3,2},{4,5},{5,4},{6,7},{7,6},{8,9},{9,8},{10,11... | collective-permute-start | bytes 1179656 | tf_op jit(solution)/shard_map/ppermute | solution.py:28
  29.3 1.3 %copy-start = (bf16[768,768]{1,0:T(8,128)(2,1)S(1)}, bf16[768,768]{1,0:T(8,128)(2,1)}, u32[]{:S(2)}) copy-start(bf16[768,768]{1,0:T(8,128)(2,1)} %refs_2_.1) | copy-start | bytes 3538948
  30.6 1.0 copy-start.2
  31.6 0.7 copy-start.4
  32.3 6.5 %copy-start.5 = (bf16[256,768]{1,0:T(8,128)(2,1)S(1)}, bf16[256,768]{1,0:T(8,128)(2,1)}, u32[]{:S(2)}) copy-start(bf16[256,768]{1,0:T(8,128)(2,1)} %text_ref.1) | copy-start | bytes 1179652
  35.3 5.9 %collective-permute-start.2 = (bf16[256,768]{1,0:T(8,128)(2,1)}, bf16[256,768]{1,0:T(8,128)(2,1)S(1)}, u32[]{:S(2)}, u32[]{:S(2)}) collective-permute-start(bf16[256,768]{1,0:T(8,128)(2,1)} %broadcast_select_fusion.1), channel_id=1, source_target_pairs={{0,1},{1,0},{2,3},{3,2},{4,5},{5,4},{6,7},{7,6},{8,9},{9,8},{10,11... | collective-permute-start | bytes 1179656 | tf_op jit(solution)/shard_map/ppermute | solution.py:28
  38.8 2.5 %copy-start.3 = (bf16[256,768]{1,0:T(8,128)(2,1)S(1)}, bf16[256,768]{1,0:T(8,128)(2,1)}, u32[]{:S(2)}) copy-start(bf16[256,768]{1,0:T(8,128)(2,1)} %feats_ref.1) | copy-start | bytes 1179652
  44.0 28.9 %all-to-all-start = ((bf16[16,48,768]{2,1,0:T(8,128)(2,1)}), bf16[16,48,768]{2,1,0:T(8,128)(2,1)S(1)}, u32[]{:S(2)}, u32[]{:S(2)}) async-start(bf16[16,48,768]{2,1,0:T(8,128)(2,1)} %bitcast.4), calls=%async_computation | async-start | bytes 2359296 | tf_op jit(solution)/shard_map/all_to_all | solution.py:171
  47.6 52.4 %collective-permute-start.6 = (bf16[272,768]{1,0:T(8,128)(2,1)S(1)}, bf16[272,768]{1,0:T(8,128)(2,1)S(1)}, u32[]{:S(2)}, u32[]{:S(2)}) collective-permute-start(bf16[272,768]{1,0:T(8,128)(2,1)S(1)} %get-tuple-element.25.parcel_ref.own_ref), channel_id=1, source_target_pairs={{1022,0},{1023,1},{0,2},{1,3},{2,4},{3,5},{4,6},{5,7},{6,8},{7,9},... | collective-permute-start | bytes 1253384 | tf_op jit(solution)/shard_map/ppermute | solution.py:24
  50.8 49.2 %collective-permute-start.5 = (bf16[272,768]{1,0:T(8,128)(2,1)S(1)}, bf16[272,768]{1,0:T(8,128)(2,1)S(1)}, u32[]{:S(2)}, u32[]{:S(2)}) collective-permute-start(bf16[272,768]{1,0:T(8,128)(2,1)S(1)} %get-tuple-element.25.parcel_ref.own_ref), channel_id=1, source_target_pairs={{2,0},{3,1},{4,2},{5,3},{6,4},{7,5},{8,6},{9,7},{10,8},{11,9},{12,... | collective-permute-start | bytes 1253384 | tf_op jit(solution)/shard_map/ppermute | solution.py:24
  62.0 43.1 %collective-permute-start.4 = (bf16[272,768]{1,0:T(8,128)(2,1)S(1)}, bf16[272,768]{1,0:T(8,128)(2,1)S(1)}, u32[]{:S(2)}, u32[]{:S(2)}) collective-permute-start(bf16[272,768]{1,0:T(8,128)(2,1)S(1)} %get-tuple-element.25.parcel_ref.own_ref), channel_id=1, source_target_pairs={{0,1},{1,0},{2,3},{3,2},{4,5},{5,4},{6,7},{7,6},{8,9},{9,8},{10,11... | collective-permute-start | bytes 1253384 | tf_op jit(solution)/shard_map/ppermute | solution.py:28
  73.3 30.6 %copy-start.1 = (bf16[768,768]{1,0:T(8,128)(2,1)S(1)}, bf16[768,768]{1,0:T(8,128)(2,1)}, u32[]{:S(2)}) copy-start(bf16[768,768]{1,0:T(8,128)(2,1)} %refs_2_.1) | copy-start | bytes 3538948
  74.3 38.2 %all-to-all-start.1 = ((bf16[64,8,72]{2,1,0:T(8,128)(2,1)}), bf16[64,8,72]{2,1,0:T(8,128)(2,1)S(1)}, u32[]{:S(2)}, u32[]{:S(2)}) async-start(bf16[64,8,72]{2,1,0:T(8,128)(2,1)} %reshape.46), calls=%async_computation.1 | async-start | bytes 262144 | tf_op jit(solution)/shard_map/all_to_all | solution.py:185
  100.1 5.2 %copy-start.6 = (bf16[256,768]{1,0:T(8,128)(2,1)S(1)}, bf16[256,768]{1,0:T(8,128)(2,1)}, u32[]{:S(2)}) copy-start(bf16[256,768]{1,0:T(8,128)(2,1)} %text_ref.1) | copy-start | bytes 1179652
  100.1 5.1 %collective-permute-start.7 = (bf16[272,768]{1,0:T(8,128)(2,1)S(1)}, bf16[272,768]{1,0:T(8,128)(2,1)S(1)}, u32[]{:S(2)}, u32[]{:S(2)}) collective-permute-start(bf16[272,768]{1,0:T(8,128)(2,1)S(1)} %broadcast_select_fusion), channel_id=1, source_target_pairs={{0,1},{1,0},{2,3},{3,2},{4,5},{5,4},{6,7},{7,6},{8,9},{9,8},{10,11... | collective-permute-start | bytes 1253384 | tf_op jit(solution)/shard_map/ppermute | solution.py:28

commit v3 on v2

--- a/solution.py
+++ b/solution.py
@@ -45,7 +45,7 @@
         in_specs=[SMEM] * scalars + [VMEM] * (len(args) - scalars),
         out_specs=[VMEM] * len(outs),
         compiler_params=pltpu.CompilerParams(vmem_limit_bytes=32 * 2**20),
-        cost_estimate=pl.CostEstimate(flops=flops, bytes_accessed=moved, transcendentals=0),
+        cost_estimate=pl.CostEstimate(flops=flops, bytes_accessed=moved if flops else 0, transcendentals=0),
     )(*args)
 
 
@@ -66,12 +66,12 @@
     parcel_ref[rows:, :rows] = codes.astype(F32).astype(BF16)
 
 
-def pair_terms(text, parcel_ref, place, with_loss=True):
+def pair_terms(text, parcel, place, with_loss=True):
     rows = text.shape[0]
-    codes = parcel_ref[rows:, :rows].astype(F32)
+    codes = parcel[rows:, :rows].astype(F32)
     target = (codes[0:1] - (place + HALF)) * rows + codes[1:2]
     match = lax.broadcasted_iota(jnp.int32, (rows, rows), 0).astype(F32) == target
-    logit = TEMP * dot(text, parcel_ref[:rows, :], ((1,), (1,))) + BIAS
+    logit = TEMP * dot(text, parcel[:rows], ((1,), (1,))) + BIAS
     z = jnp.where(match, -logit, logit)
     small = jnp.exp(-jnp.abs(z))
     share = 1.0 / (1.0 + small)
@@ -85,10 +85,11 @@
 
 def image_start(side_ref, parcel_ref, own_ref, mate_ref, ahead_ref, behind_ref, grad_ref, loss_ref):
     side = side_ref[0].astype(F32)
+    parcel = parcel_ref[...]
     grad, total = None, None
     for text_ref, place in ((own_ref, 0), (mate_ref, side), (ahead_ref, HALF), (behind_ref, -HALF)):
         text = text_ref[...]
-        slope, loss = pair_terms(text, parcel_ref, place)
+        slope, loss = pair_terms(text, parcel, place)
         part = dot(slope, text, ((0,), (0,)))
         grad, total = (part, loss) if grad is None else (grad + part, total + loss)
     grad_ref[...] = grad
@@ -100,7 +101,7 @@
 ):
     half = feats_ref.shape[1] // 2
     far = far_ref[...]
-    slope, loss = pair_terms(far, parcel_ref, -side_ref[0].astype(F32))
+    slope, loss = pair_terms(far, parcel_ref[...], -side_ref[0].astype(F32))
     out_loss_ref[...] = loss_ref[...] + loss
     unit_grad = TEMP * (grad_ref[...] + dot(slope, far, ((0,), (0,))))
     proj = proj_ref[...]
@@ -113,16 +114,21 @@
     terms_ref[:, half:] = dot(back, feats_ref[:, :half], ((0,), (0,))).astype(BF16)
 
 
-def text_side(side_ref, text_ref, own_ref, mate_ref, ahead_ref, behind_ref, far_ref, grad_ref):
+def text_side(side_ref, text_ref, mate_ref, own_ref, ahead_ref, behind_ref, grad_ref, mate_grad_ref):
     rows = text_ref.shape[0]
     side = side_ref[0].astype(F32)
-    text = text_ref[...]
-    grad = None
-    for parcel_ref, place in ((own_ref, 0), (mate_ref, -side), (ahead_ref, -HALF), (behind_ref, HALF), (far_ref, side)):
-        slope = pair_terms(text, parcel_ref, place, with_loss=False)
-        part = dot(slope, parcel_ref[:rows, :], ((1,), (0,)))
-        grad = part if grad is None else grad + part
-    grad_ref[...] = TEMP * grad
+    own, ahead, behind = own_ref[...], ahead_ref[...], behind_ref[...]
+    near = jnp.where(side > 0, ahead, behind)
+
+    def total(text, parcels):
+        parts = [
+            dot(pair_terms(text, parcel, place, with_loss=False), parcel[:rows], ((1,), (0,)))
+            for parcel, place in parcels
+        ]
+        return sum(parts[1:], parts[0])
+
+    mate_grad_ref[...] = total(mate_ref[...], [(own, side), (near, -side)]).astype(BF16)
+    grad_ref[...] = total(text_ref[...], [(own, 0), (ahead, -HALF), (behind, HALF)])
 
 
 def local(image_feats, text_emb, head_weight, partner):
@@ -145,45 +151,44 @@
         product,
         1,
     )
+    parcel_ahead, parcel_behind = from_ahead(parcel, HALF), from_ahead(parcel, -HALF)
     ahead, behind, parcel = lax.optimization_barrier((ahead, behind, parcel))
     far = other_core(jnp.where(core == 0, ahead, behind))
     grad, loss = kernel_call(
         image_start,
         [shape((rows, width), F32), shape((1, rows), F32)],
         [side, parcel, text_emb, mate, ahead, behind],
-        8 * pair,
+        0,
         1,
     )
     proj_grad, terms, row_loss = kernel_call(
         image_end,
         [shape((rows, width), BF16), shape((width, width), BF16), shape((1, rows), F32)],
         [side, parcel, far, proj, grad, loss, image_feats],
-        2 * pair + product,
-        1,
-    )
-    sent = after(parcel, terms)
-    parcel_ahead, parcel_behind = from_ahead(sent, HALF), from_ahead(sent, -HALF)
-    parcel_mate = other_core(sent)
-    parcel_far = other_core(jnp.where(core == 0, parcel_ahead, parcel_behind))
+        0,
+        1,
+    )
+    terms = after(terms, parcel_ahead, parcel_behind)
 
     n_col, n_row = lax.axis_size(COL), lax.axis_size(ROW)
     cols, tall = width // n_col, width // n_row
     mine = lax.all_to_all(terms.reshape(n_col, cols, width), COL, 0, 0, tiled=True)
 
-    (text_grad,) = kernel_call(
+    text_part, mate_part = kernel_call(
         text_side,
-        [shape((rows, width), F32)],
-        [side, text_emb, parcel, parcel_mate, parcel_ahead, parcel_behind, parcel_far],
+        [shape((rows, width), F32), shape((rows, width), BF16)],
+        [side, after(text_emb, proj_grad), mate, parcel, parcel_ahead, parcel_behind],
         10 * pair,
         1,
     )
+    text_grad = TEMP * (text_part + other_core(mate_part).astype(F32))
     feat_grad = dot(proj_grad, head_weight, ((1,), (1,))).astype(BF16)
 
     pick = jnp.tile(jnp.eye(cols, dtype=BF16), (n_col, 1))
     summed = dot(mine.reshape(width, width), pick, ((0,), (0,))).astype(BF16)
     order = [(i + n_row // 2) % n_row for i in range(n_row)]
     last = lax.all_to_all(
-        summed.reshape(n_row, 8, tall * cols // 8), ROW, 0, 0, axis_index_groups=[order], tiled=True
+        summed.reshape(n_row, 2, tall * cols // 2), ROW, 0, 0, axis_index_groups=[order], tiled=True
     )
     head_grad = jnp.sum(last.astype(F32), axis=0).reshape(tall, cols)
     return row_loss.reshape(rows), feat_grad, text_grad, head_grad

time: 114 us -> 120 us (1.053)
  waiting for transfers between devices: 14.3 us -> 27.2 us
  starting transfers between devices: 82.1 us -> 71.2 us
  Pallas kernels: 8.79 us -> 10.1 us
  matrix products: 1.6 us -> 2.86 us
    ppermute x4 -> x3, starting transfers between devices: 12.6 us -> 7.5 us  [other_core(): return lax.ppermute(block, CORE, [(0, 1), (1, 0)])]
    all_to_all x1, waiting for transfers between devices: 8.31 us -> 13.2 us  [local(): lax.all_to_all(terms.reshape(n_col, cols, width), COL, 0, 0, tiled=True)]
    ppermute x4, waiting for transfers between devices: 1.65 us -> 6.26 us  [from_ahead(): lax.ppermute(block, LOOP, [((i + distance) % n, i) for i in range(n)])]
    all_to_all x1, starting transfers between devices: 25.7 us -> 21.7 us  [local(): lax.all_to_all(summed.reshape(n_row, 2, tall * cols // 2), ROW, 0, 0, axi...]
    all_to_all x1, waiting for transfers between devices: 4.24 us -> 7.72 us  [local(): lax.all_to_all(summed.reshape(n_row, 2, tall * cols // 2), ROW, 0, 0, axi...]
    ppermute x4, starting transfers between devices: 40.2 us -> 36.8 us  [from_ahead(): lax.ppermute(block, LOOP, [((i + distance) % n, i) for i in range(n)])]
    all_to_all x1, starting transfers between devices: 3.6 us -> 5.23 us  [local(): lax.all_to_all(terms.reshape(n_col, cols, width), COL, 0, 0, tiled=True)]
    dot_general x2, matrix products: 1.6 us -> 2.86 us  [dot(): return lax.dot_general(a, b, (dims, ((), ())), preferred_element_type=F32)]
  transfers between devices with their start and end apart: 10 -> 9, of which waited for: 5 -> 3; matrix products, arithmetic and copies ran while one was open for 3% -> 5% of each run, Pallas kernels for 5% -> 8%
where the time goes in v3:
time: 120 us
  starting transfers between devices  71.2 us (59%)
  waiting for transfers between devices  27.2 us (23%)
  Pallas kernels  10.1 us (8%)
  local copies, waits for them, and re-layouts  5.48 us (5%)
  matrix products  2.86 us (2%)
  other arithmetic  1.88 us (2%)
    ppermute x4, starting transfers between devices, from_ahead(): lax.ppermute(block, LOOP, [((i + distance) % n, i) for i in range(n)])  36.8 us
    all_to_all x1, starting transfers between devices, local(): lax.all_to_all(summed.reshape(n_row, 2, tall * cols // 2), ROW, 0, 0, axi...  21.7 us
    all_to_all x1, waiting for transfers between devices, local(): lax.all_to_all(terms.reshape(n_col, cols, width), COL, 0, 0, tiled=True)  13.2 us
    pallas_call x4, Pallas kernels, kernel_call(): pl.pallas_call(body, out_shape=outs, in_specs=[SMEM] * scalars + [VMEM] *...  10.1 us
    all_to_all x1, waiting for transfers between devices, local(): lax.all_to_all(summed.reshape(n_row, 2, tall * cols // 2), ROW, 0, 0, axi...  7.72 us
    ppermute x3, starting transfers between devices, other_core(): return lax.ppermute(block, CORE, [(0, 1), (1, 0)])  7.5 us
    ppermute x4, waiting for transfers between devices, from_ahead(): lax.ppermute(block, LOOP, [((i + distance) % n, i) for i in range(n)])  6.26 us
    all_to_all x1, starting transfers between devices, local(): lax.all_to_all(terms.reshape(n_col, cols, width), COL, 0, 0, tiled=True)  5.23 us
  transfers between devices with their start and end apart: 9, of which 3 were waited for; matrix products, arithmetic and copies ran while one was open for 5% of the time, Pallas kernels for 8%

profile of v3, /device:TPU:1, one launch (start us, length us, event | category | flops | bytes accessed | tf_op | source)
XLA Modules:
  0.0 119.6 jit_solution(13897311200392435250)
XLA Ops:
  0.6 23.9 %collective-permute-start = (bf16[256,768]{1,0:T(8,128)(2,1)}, bf16[256,768]{1,0:T(8,128)(2,1)S(1)}, u32[]{:S(2)}, u32[]{:S(2)}) collective-permute-start(bf16[256,768]{1,0:T(8,128)(2,1)} %text_ref), channel_id=1, source_target_pairs={{2,0},{3,1},{4,2},{5,3},{6,4},{7,5},{8,6},{9,7},{10,8},{11,9},{12,... | collective-permute-start | bytes 1179656 | tf_op jit(solution)/shard_map/ppermute | solution.py:24
  24.5 1.9 %collective-permute-start.1 = (bf16[256,768]{1,0:T(8,128)(2,1)}, bf16[256,768]{1,0:T(8,128)(2,1)S(1)}, u32[]{:S(2)}, u32[]{:S(2)}) collective-permute-start(bf16[256,768]{1,0:T(8,128)(2,1)} %text_ref), channel_id=1, source_target_pairs={{1022,0},{1023,1},{0,2},{1,3},{2,4},{3,5},{4,6},{5,7},{6,8},{7,9},... | collective-permute-start | bytes 1179656 | tf_op jit(solution)/shard_map/ppermute | solution.py:24
  26.4 2.9 %collective-permute-start.3 = (bf16[256,768]{1,0:T(8,128)(2,1)}, bf16[256,768]{1,0:T(8,128)(2,1)S(1)}, u32[]{:S(2)}, u32[]{:S(2)}) collective-permute-start(bf16[256,768]{1,0:T(8,128)(2,1)} %text_ref), channel_id=1, source_target_pairs={{0,1},{1,0},{2,3},{3,2},{4,5},{5,4},{6,7},{7,6},{8,9},{9,8},{10,11... | collective-permute-start | bytes 1179656 | tf_op jit(solution)/shard_map/ppermute | solution.py:28
  29.3 0.0 copy-start
  29.3 1.3 %copy-done = bf16[768,768]{1,0:T(8,128)(2,1)S(1)} copy-done((bf16[768,768]{1,0:T(8,128)(2,1)S(1)}, bf16[768,768]{1,0:T(8,128)(2,1)}, u32[]{:S(2)}) %copy-start) | copy-done | bytes 1179672
  30.6 0.0 copy-start.2
  30.6 1.0 copy-done.2
  31.6 0.0 copy-start.7
  31.6 0.7 copy-done.7
  32.3 0.0 copy-start.4
  32.3 0.6 shard_map.75
  32.9 9.1 %collective-permute-start.4 = (bf16[272,768]{1,0:T(8,128)(2,1)S(1)}, bf16[272,768]{1,0:T(8,128)(2,1)}, u32[]{:S(2)}, u32[]{:S(2)}) collective-permute-start(bf16[272,768]{1,0:T(8,128)(2,1)S(1)} %get-tuple-element.19.parcel_ref.own_ref), channel_id=1, source_target_pairs={{2,0},{3,1},{4,2},{5,3},{6,4},{7,5},{8,6},{9,7},{10,8},{11,9},{12,... | collective-permute-start | bytes 1253384 | tf_op jit(solution)/shard_map/ppermute | solution.py:24
  41.9 1.9 %collective-permute-start.5 = (bf16[272,768]{1,0:T(8,128)(2,1)S(1)}, bf16[272,768]{1,0:T(8,128)(2,1)}, u32[]{:S(2)}, u32[]{:S(2)}) collective-permute-start(bf16[272,768]{1,0:T(8,128)(2,1)S(1)} %get-tuple-element.19.parcel_ref.own_ref), channel_id=1, source_target_pairs={{1022,0},{1023,1},{0,2},{1,3},{2,4},{3,5},{4,6},{5,7},{6,8},{7,9},... | collective-permute-start | bytes 1253384 | tf_op jit(solution)/shard_map/ppermute | solution.py:24
  43.9 0.0 collective-permute-done.ahead_ref
  43.9 0.0 collective-permute-done.1.behind_ref
  43.9 0.8 broadcast_select_fusion
  44.7 0.0 copy-start.3
  44.7 2.3 %collective-permute-start.2 = (bf16[256,768]{1,0:T(8,128)(2,1)}, bf16[256,768]{1,0:T(8,128)(2,1)}, u32[]{:S(2)}, u32[]{:S(2)}) collective-permute-start(bf16[256,768]{1,0:T(8,128)(2,1)} %broadcast_select_fusion), channel_id=1, source_target_pairs={{0,1},{1,0},{2,3},{3,2},{4,5},{5,4},{6,7},{7,6},{8,9},{9,8},{10,11... | collective-permute-start | bytes 1179656 | tf_op jit(solution)/shard_map/ppermute | solution.py:28
  47.0 0.0 collective-permute-done.3.mate_ref
  47.0 0.0 copy-done.4
  47.0 2.4 %shard_map.76 = (f32[256,768]{1,0:T(8,128)S(1)}, f32[1,256]{1,0:T(1,128)S(1)}) custom-call(s32[1]{0:T(128)} %bitcast.side_ref, bf16[272,768]{1,0:T(8,128)(2,1)S(1)} %get-tuple-element.19.parcel_ref.own_ref, bf16[256,768]{1,0:T(8,128)(2,1)S(1)} %copy-done.4, bf16[256,768]{1,0:T(8,128)(2,1)S(1)} %collective-permute-done.3.mate_ref, ...), custom_call_target="tpu_custom_call" | custom-call | tf_op jit(solution)/shard_map/pallas_call | solution.py:42
  49.5 0.0 collective-permute-done.2.far_ref
  49.5 0.0 copy-done.3
  49.5 3.8 %shard_map.77 = (bf16[256,768]{1,0:T(8,128)(2,1)S(1)}, bf16[768,768]{1,0:T(8,128)(2,1)}, f32[1,256]{1,0:T(1,128)}) custom-call(s32[1]{0:T(128)} %bitcast.side_ref, bf16[272,768]{1,0:T(8,128)(2,1)S(1)} %get-tuple-element.19.parcel_ref.own_ref, bf16[256,768]{1,0:T(8,128)(2,1)} %collective-permute-done.2.far_ref, f32[256,768]{1,0:T(8,128)S(1)} %get-tuple-element.22.proj_ref, ...), custom_call_target="tpu_custom_call" | custom-call | tf_op jit(solution)/shard_map/pallas_call | solution.py:42
  53.3 0.0 copy-start.5
  53.3 0.7 copy-done.5
  54.1 0.0 collective-permute-done.4.ahead_ref
  54.1 6.3 %collective-permute-done.5.behind_ref = bf16[272,768]{1,0:T(8,128)(2,1)} collective-permute-done((bf16[272,768]{1,0:T(8,128)(2,1)S(1)}, bf16[272,768]{1,0:T(8,128)(2,1)}, u32[]{:S(2)}, u32[]{:S(2)}) %collective-permute-start.5) | collective-permute-done | bytes 417824 | tf_op jit(solution)/shard_map/ppermute | solution.py:24
  60.3 5.2 %all-to-all-start = ((bf16[16,48,768]{2,1,0:T(8,128)(2,1)}), bf16[16,48,768]{2,1,0:T(8,128)(2,1)}, u32[]{:S(2)}, u32[]{:S(2)}) async-start(bf16[16,48,768]{2,1,0:T(8,128)(2,1)} %bitcast.4), calls=%async_computation | async-start | bytes 2359296 | tf_op jit(solution)/shard_map/all_to_all | solution.py:175
  65.6 3.2 %shard_map.78 = (f32[256,768]{1,0:T(8,128)S(1)}, bf16[256,768]{1,0:T(8,128)(2,1)}) custom-call(s32[1]{0:T(128)} %bitcast.side_ref, bf16[256,768]{1,0:T(8,128)(2,1)S(1)} %copy-done.4, bf16[256,768]{1,0:T(8,128)(2,1)S(1)} %collective-permute-done.3.mate_ref, bf16[272,768]{1,0:T(8,128)(2,1)S(1)} %get-tuple-element.19.parcel_ref.own_ref, ...), custom_call_target="tpu_custom_call" | custom-call | flops 1006632960 | bytes 3219460 | tf_op jit(solution)/shard_map/pallas_call | solution.py:42
  68.8 0.0 copy-start.1
  68.8 0.0 copy-start.6
  68.8 2.3 %collective-permute-start.6 = (bf16[256,768]{1,0:T(8,128)(2,1)}, bf16[256,768]{1,0:T(8,128)(2,1)S(1)}, u32[]{:S(2)}, u32[]{:S(2)}) collective-permute-start(bf16[256,768]{1,0:T(8,128)(2,1)} %get-tuple-element.29), channel_id=1, source_target_pairs={{0,1},{1,0},{2,3},{3,2},{4,5},{5,4},{6,7},{7,6},{8,9},{9,8},{10,11... | collective-permute-start | bytes 1179656 | tf_op jit(solution)/shard_map/ppermute | solution.py:28
  71.1 13.2 %all-to-all-done = bf16[16,48,768]{2,1,0:T(8,128)(2,1)} async-done(((bf16[16,48,768]{2,1,0:T(8,128)(2,1)}), bf16[16,48,768]{2,1,0:T(8,128)(2,1)}, u32[]{:S(2)}, u32[]{:S(2)}) %all-to-all-start) | async-done | bytes 1179680 | tf_op jit(solution)/shard_map/all_to_all | solution.py:175
  84.4 1.6 %fusion = bf16[768,48]{0,1:T(8,128)(2,1)S(1)} fusion(bf16[16,48,768]{2,1,0:T(8,128)(2,1)} %all-to-all-done, bf16[48,48]{0,1:T(8,128)(2,1)S(1)} %fusion.2), kind=kOutput, calls=%fused_computation.2 | convolution fusion | flops 56659968 | bytes 1257984 | tf_op jit(solution)/shard_map/dot_general | solution.py:36
  86.0 0.2 copy.8
  86.2 0.9 reshape.46
  87.1 21.7 %all-to-all-start.1 = ((bf16[64,2,288]{2,1,0:T(2,128)(2,1)}), bf16[64,2,288]{2,1,0:T(2,128)(2,1)S(1)}, u32[]{:S(2)}, u32[]{:S(2)}) async-start(bf16[64,2,288]{2,1,0:T(2,128)(2,1)} %reshape.46), calls=%async_computation.1 | async-start | bytes 196608 | tf_op jit(solution)/shard_map/all_to_all | solution.py:190
  108.8 0.0 copy-done.1
  108.8 0.0 copy-done.6
  108.8 1.3 %convolution_convert_fusion = bf16[256,768]{1,0:T(8,128)(2,1)} fusion(bf16[256,768]{1,0:T(8,128)(2,1)S(1)} %copy-done.6, bf16[768,768]{1,0:T(8,128)(2,1)S(1)} %copy-done.1), kind=kOutput, calls=%fused_computation | convolution fusion | flops 302186496 | bytes 1966080 | tf_op jit(solution)/shard_map/dot_general | solution.py:36
  110.1 0.0 collective-permute-done.6
  110.1 1.0 add_multiply_fusion
  111.1 7.7 %all-to-all-done.1 = bf16[64,2,288]{2,1,0:T(2,128)(2,1)S(1)} async-done(((bf16[64,2,288]{2,1,0:T(2,128)(2,1)}), bf16[64,2,288]{2,1,0:T(2,128)(2,1)S(1)}, u32[]{:S(2)}, u32[]{:S(2)}) %all-to-all-start.1) | async-done | bytes 73760 | tf_op jit(solution)/shard_map/all_to_all | solution.py:190
  118.8 0.1 convert_reduce_fusion
  118.9 0.7 reshape.47
  (1 shorter events, 0.0 us)
Async XLA Ops:
  0.6 43.2 %collective-permute-start = (bf16[256,768]{1,0:T(8,128)(2,1)}, bf16[256,768]{1,0:T(8,128)(2,1)S(1)}, u32[]{:S(2)}, u32[]{:S(2)}) collective-permute-start(bf16[256,768]{1,0:T(8,128)(2,1)} %text_ref), channel_id=1, source_target_pairs={{2,0},{3,1},{4,2},{5,3},{6,4},{7,5},{8,6},{9,7},{10,8},{11,9},{12,... | collective-permute-start | bytes 1179656 | tf_op jit(solution)/shard_map/ppermute | solution.py:24
  24.5 19.4 %collective-permute-start.1 = (bf16[256,768]{1,0:T(8,128)(2,1)}, bf16[256,768]{1,0:T(8,128)(2,1)S(1)}, u32[]{:S(2)}, u32[]{:S(2)}) collective-permute-start(bf16[256,768]{1,0:T(8,128)(2,1)} %text_ref), channel_id=1, source_target_pairs={{1022,0},{1023,1},{0,2},{1,3},{2,4},{3,5},{4,6},{5,7},{6,8},{7,9},... | collective-permute-start | bytes 1179656 | tf_op jit(solution)/shard_map/ppermute | solution.py:24
  26.4 20.6 %collective-permute-start.3 = (bf16[256,768]{1,0:T(8,128)(2,1)}, bf16[256,768]{1,0:T(8,128)(2,1)S(1)}, u32[]{:S(2)}, u32[]{:S(2)}) collective-permute-start(bf16[256,768]{1,0:T(8,128)(2,1)} %text_ref), channel_id=1, source_target_pairs={{0,1},{1,0},{2,3},{3,2},{4,5},{5,4},{6,7},{7,6},{8,9},{9,8},{10,11... | collective-permute-start | bytes 1179656 | tf_op jit(solution)/shard_map/ppermute | solution.py:28
  29.3 1.3 %copy-start = (bf16[768,768]{1,0:T(8,128)(2,1)S(1)}, bf16[768,768]{1,0:T(8,128)(2,1)}, u32[]{:S(2)}) copy-start(bf16[768,768]{1,0:T(8,128)(2,1)} %refs_2_.1) | copy-start | bytes 3538948
  30.6 1.0 copy-start.2
  31.6 0.7 copy-start.7
  32.3 14.8 %copy-start.4 = (bf16[256,768]{1,0:T(8,128)(2,1)S(1)}, bf16[256,768]{1,0:T(8,128)(2,1)}, u32[]{:S(2)}) copy-start(bf16[256,768]{1,0:T(8,128)(2,1)} %text_ref) | copy-start | bytes 1179652
  32.9 21.2 %collective-permute-start.4 = (bf16[272,768]{1,0:T(8,128)(2,1)S(1)}, bf16[272,768]{1,0:T(8,128)(2,1)}, u32[]{:S(2)}, u32[]{:S(2)}) collective-permute-start(bf16[272,768]{1,0:T(8,128)(2,1)S(1)} %get-tuple-element.19.parcel_ref.own_ref), channel_id=1, source_target_pairs={{2,0},{3,1},{4,2},{5,3},{6,4},{7,5},{8,6},{9,7},{10,8},{11,9},{12,... | collective-permute-start | bytes 1253384 | tf_op jit(solution)/shard_map/ppermute | solution.py:24
  41.9 18.4 %collective-permute-start.5 = (bf16[272,768]{1,0:T(8,128)(2,1)S(1)}, bf16[272,768]{1,0:T(8,128)(2,1)}, u32[]{:S(2)}, u32[]{:S(2)}) collective-permute-start(bf16[272,768]{1,0:T(8,128)(2,1)S(1)} %get-tuple-element.19.parcel_ref.own_ref), channel_id=1, source_target_pairs={{1022,0},{1023,1},{0,2},{1,3},{2,4},{3,5},{4,6},{5,7},{6,8},{7,9},... | collective-permute-start | bytes 1253384 | tf_op jit(solution)/shard_map/ppermute | solution.py:24
  44.7 4.8 %copy-start.3 = (bf16[256,768]{1,0:T(8,128)(2,1)S(1)}, bf16[256,768]{1,0:T(8,128)(2,1)}, u32[]{:S(2)}) copy-start(bf16[256,768]{1,0:T(8,128)(2,1)} %feats_ref.1) | copy-start | bytes 1179652
  44.7 4.8 %collective-permute-start.2 = (bf16[256,768]{1,0:T(8,128)(2,1)}, bf16[256,768]{1,0:T(8,128)(2,1)}, u32[]{:S(2)}, u32[]{:S(2)}) collective-permute-start(bf16[256,768]{1,0:T(8,128)(2,1)} %broadcast_select_fusion), channel_id=1, source_target_pairs={{0,1},{1,0},{2,3},{3,2},{4,5},{5,4},{6,7},{7,6},{8,9},{9,8},{10,11... | collective-permute-start | bytes 1179656 | tf_op jit(solution)/shard_map/ppermute | solution.py:28
  53.3 0.7 copy-start.5
  60.3 24.1 %all-to-all-start = ((bf16[16,48,768]{2,1,0:T(8,128)(2,1)}), bf16[16,48,768]{2,1,0:T(8,128)(2,1)}, u32[]{:S(2)}, u32[]{:S(2)}) async-start(bf16[16,48,768]{2,1,0:T(8,128)(2,1)} %bitcast.4), calls=%async_computation | async-start | bytes 2359296 | tf_op jit(solution)/shard_map/all_to_all | solution.py:175
  68.8 40.0 %copy-start.1 = (bf16[768,768]{1,0:T(8,128)(2,1)S(1)}, bf16[768,768]{1,0:T(8,128)(2,1)}, u32[]{:S(2)}) copy-start(bf16[768,768]{1,0:T(8,128)(2,1)} %refs_2_.1) | copy-start | bytes 3538948
  68.8 40.0 %copy-start.6 = (bf16[256,768]{1,0:T(8,128)(2,1)S(1)}, bf16[256,768]{1,0:T(8,128)(2,1)}, u32[]{:S(2)}) copy-start(bf16[256,768]{1,0:T(8,128)(2,1)} %copy-done.5) | copy-start | bytes 1179652
  68.8 41.3 %collective-permute-start.6 = (bf16[256,768]{1,0:T(8,128)(2,1)}, bf16[256,768]{1,0:T(8,128)(2,1)S(1)}, u32[]{:S(2)}, u32[]{:S(2)}) collective-permute-start(bf16[256,768]{1,0:T(8,128)(2,1)} %get-tuple-element.29), channel_id=1, source_target_pairs={{0,1},{1,0},{2,3},{3,2},{4,5},{5,4},{6,7},{7,6},{8,9},{9,8},{10,11... | collective-permute-start | bytes 1179656 | tf_op jit(solution)/shard_map/ppermute | solution.py:28
  87.1 31.7 %all-to-all-start.1 = ((bf16[64,2,288]{2,1,0:T(2,128)(2,1)}), bf16[64,2,288]{2,1,0:T(2,128)(2,1)S(1)}, u32[]{:S(2)}, u32[]{:S(2)}) async-start(bf16[64,2,288]{2,1,0:T(2,128)(2,1)} %reshape.46), calls=%async_computation.1 | async-start | bytes 196608 | tf_op jit(solution)/shard_map/all_to_all | solution.py:190

commit v4 on v3

--- a/solution.py
+++ b/solution.py
@@ -44,7 +44,7 @@
         out_shape=outs,
         in_specs=[SMEM] * scalars + [VMEM] * (len(args) - scalars),
         out_specs=[VMEM] * len(outs),
-        compiler_params=pltpu.CompilerParams(vmem_limit_bytes=32 * 2**20),
+        compiler_params=pltpu.CompilerParams(vmem_limit_bytes=16 * 2**20),
         cost_estimate=pl.CostEstimate(flops=flops, bytes_accessed=moved if flops else 0, transcendentals=0),
     )(*args)
 
@@ -151,21 +151,23 @@
         product,
         1,
     )
-    parcel_ahead, parcel_behind = from_ahead(parcel, HALF), from_ahead(parcel, -HALF)
     ahead, behind, parcel = lax.optimization_barrier((ahead, behind, parcel))
-    far = other_core(jnp.where(core == 0, ahead, behind))
+    near = jnp.where(core == 0, ahead, behind)
+    far = other_core(near)
+    sent = after(parcel, near)
+    parcel_ahead, parcel_behind = from_ahead(sent, HALF), from_ahead(sent, -HALF)
     grad, loss = kernel_call(
         image_start,
         [shape((rows, width), F32), shape((1, rows), F32)],
         [side, parcel, text_emb, mate, ahead, behind],
-        0,
+        8 * pair,
         1,
     )
     proj_grad, terms, row_loss = kernel_call(
         image_end,
         [shape((rows, width), BF16), shape((width, width), BF16), shape((1, rows), F32)],
         [side, parcel, far, proj, grad, loss, image_feats],
-        0,
+        2 * pair + product,
         1,
     )
     terms = after(terms, parcel_ahead, parcel_behind)

time: 120 us -> 122 us (1.017)
  starting transfers between devices: 71.2 us -> 75.8 us
  waiting for transfers between devices: 27.2 us -> 25.5 us
    all_to_all x1, starting transfers between devices: 21.7 us -> 25 us  [local(): lax.all_to_all(summed.reshape(n_row, 2, tall * cols // 2), ROW, 0, 0, axi...]
    ppermute x4, waiting for transfers between devices: 6.26 us -> 4.47 us  [from_ahead(): lax.ppermute(block, LOOP, [((i + distance) % n, i) for i in range(n)])]
    unnamed x16 -> x14, local copies, waits for them, and re-layouts: 3.7 us -> 2.96 us
  transfers between devices with their start and end apart: 9 -> 9, of which waited for: 3 -> 6; matrix products, arithmetic and copies ran while one was open for 5% -> 5% of each run, Pallas kernels for 8% -> 8%
where the time goes in v4:
time: 122 us
  starting transfers between devices  75.8 us (62%)
  waiting for transfers between devices  25.5 us (21%)
  Pallas kernels  9.94 us (8%)
  local copies, waits for them, and re-layouts  4.73 us (4%)
  matrix products  2.87 us (2%)
  other arithmetic  1.89 us (2%)
    ppermute x4, starting transfers between devices, from_ahead(): lax.ppermute(block, LOOP, [((i + distance) % n, i) for i in range(n)])  37.2 us
    all_to_all x1, starting transfers between devices, local(): lax.all_to_all(summed.reshape(n_row, 2, tall * cols // 2), ROW, 0, 0, axi...  25 us
    all_to_all x1, waiting for transfers between devices, local(): lax.all_to_all(terms.reshape(n_col, cols, width), COL, 0, 0, tiled=True)  13.3 us
    pallas_call x4, Pallas kernels, kernel_call(): pl.pallas_call(body, out_shape=outs, in_specs=[SMEM] * scalars + [VMEM] *...  9.94 us
    ppermute x3, starting transfers between devices, other_core(): return lax.ppermute(block, CORE, [(0, 1), (1, 0)])  8.63 us
    all_to_all x1, waiting for transfers between devices, local(): lax.all_to_all(summed.reshape(n_row, 2, tall * cols // 2), ROW, 0, 0, axi...  7.72 us
    all_to_all x1, starting transfers between devices, local(): lax.all_to_all(terms.reshape(n_col, cols, width), COL, 0, 0, tiled=True)  5.04 us
    ppermute x4, waiting for transfers between devices, from_ahead(): lax.ppermute(block, LOOP, [((i + distance) % n, i) for i in range(n)])  4.47 us
  transfers between devices with their start and end apart: 9, of which 6 were waited for; matrix products, arithmetic and copies ran while one was open for 5% of the time, Pallas kernels for 8%

profile of v4, /device:TPU:1, one launch (start us, length us, event | category | flops | bytes accessed | tf_op | source)
XLA Modules:
  0.0 121.5 jit_solution(14228705420941347035)
XLA Ops:
  0.6 4.0 %collective-permute-start.1 = (bf16[256,768]{1,0:T(8,128)(2,1)}, bf16[256,768]{1,0:T(8,128)(2,1)S(1)}, u32[]{:S(2)}, u32[]{:S(2)}) collective-permute-start(bf16[256,768]{1,0:T(8,128)(2,1)} %text_ref), channel_id=1, source_target_pairs={{1022,0},{1023,1},{0,2},{1,3},{2,4},{3,5},{4,6},{5,7},{6,8},{7,9},... | collective-permute-start | bytes 1179656 | tf_op jit(solution)/shard_map/ppermute | solution.py:24
  4.7 21.8 %collective-permute-start = (bf16[256,768]{1,0:T(8,128)(2,1)}, bf16[256,768]{1,0:T(8,128)(2,1)S(1)}, u32[]{:S(2)}, u32[]{:S(2)}) collective-permute-start(bf16[256,768]{1,0:T(8,128)(2,1)} %text_ref), channel_id=1, source_target_pairs={{2,0},{3,1},{4,2},{5,3},{6,4},{7,5},{8,6},{9,7},{10,8},{11,9},{12,... | collective-permute-start | bytes 1179656 | tf_op jit(solution)/shard_map/ppermute | solution.py:24
  26.4 2.9 %collective-permute-start.3 = (bf16[256,768]{1,0:T(8,128)(2,1)}, bf16[256,768]{1,0:T(8,128)(2,1)}, u32[]{:S(2)}, u32[]{:S(2)}) collective-permute-start(bf16[256,768]{1,0:T(8,128)(2,1)} %text_ref), channel_id=1, source_target_pairs={{0,1},{1,0},{2,3},{3,2},{4,5},{5,4},{6,7},{7,6},{8,9},{9,8},{10,11... | collective-permute-start | bytes 1179656 | tf_op jit(solution)/shard_map/ppermute | solution.py:28
  29.3 0.0 copy-start
  29.3 1.3 %copy-done = bf16[768,768]{1,0:T(8,128)(2,1)S(1)} copy-done((bf16[768,768]{1,0:T(8,128)(2,1)S(1)}, bf16[768,768]{1,0:T(8,128)(2,1)}, u32[]{:S(2)}) %copy-start) | copy-done | bytes 1179672
  30.6 0.0 copy-start.2
  30.6 1.0 copy-done.2
  31.6 0.0 copy-start.4
  31.6 0.7 copy-done.4
  32.3 0.0 copy-start.5
  32.3 0.6 shard_map.75
  32.9 0.7 collective-permute-done.1.behind_ref
  33.5 1.0 collective-permute-done.ahead_ref
  34.5 0.8 broadcast_select_fusion
  35.3 3.4 %collective-permute-start.2 = (bf16[256,768]{1,0:T(8,128)(2,1)}, bf16[256,768]{1,0:T(8,128)(2,1)S(1)}, u32[]{:S(2)}, u32[]{:S(2)}) collective-permute-start(bf16[256,768]{1,0:T(8,128)(2,1)} %broadcast_select_fusion), channel_id=1, source_target_pairs={{0,1},{1,0},{2,3},{3,2},{4,5},{5,4},{6,7},{7,6},{8,9},{9,8},{10,11... | collective-permute-start | bytes 1179656 | tf_op jit(solution)/shard_map/ppermute | solution.py:28
  38.8 1.9 %collective-permute-start.5 = (bf16[272,768]{1,0:T(8,128)(2,1)S(1)}, bf16[272,768]{1,0:T(8,128)(2,1)S(1)}, u32[]{:S(2)}, u32[]{:S(2)}) collective-permute-start(bf16[272,768]{1,0:T(8,128)(2,1)S(1)} %get-tuple-element.29.parcel_ref.own_ref), channel_id=1, source_target_pairs={{1022,0},{1023,1},{0,2},{1,3},{2,4},{3,5},{4,6},{5,7},{6,8},{7,9},... | collective-permute-start | bytes 1253384 | tf_op jit(solution)/shard_map/ppermute | solution.py:24
  40.7 9.4 %collective-permute-start.4 = (bf16[272,768]{1,0:T(8,128)(2,1)S(1)}, bf16[272,768]{1,0:T(8,128)(2,1)}, u32[]{:S(2)}, u32[]{:S(2)}) collective-permute-start(bf16[272,768]{1,0:T(8,128)(2,1)S(1)} %get-tuple-element.29.parcel_ref.own_ref), channel_id=1, source_target_pairs={{2,0},{3,1},{4,2},{5,3},{6,4},{7,5},{8,6},{9,7},{10,8},{11,9},{12,... | collective-permute-start | bytes 1253384 | tf_op jit(solution)/shard_map/ppermute | solution.py:24
  50.1 0.0 collective-permute-done.3.mate_ref
  50.1 0.0 copy-done.5
  50.2 0.0 copy-start.3
  50.2 3.5 %shard_map.76 = (f32[256,768]{1,0:T(8,128)S(1)}, f32[1,256]{1,0:T(1,128)S(1)}) custom-call(s32[1]{0:T(128)} %bitcast.side_ref, bf16[272,768]{1,0:T(8,128)(2,1)S(1)} %get-tuple-element.29.parcel_ref.own_ref, bf16[256,768]{1,0:T(8,128)(2,1)S(1)} %copy-done.5, bf16[256,768]{1,0:T(8,128)(2,1)} %collective-permute-done.3.mate_ref, ...), custom_call_target="tpu_custom_call" | custom-call | flops 805306368 | bytes 2778116 | tf_op jit(solution)/shard_map/pallas_call | solution.py:42
  53.6 0.0 collective-permute-done.2.far_ref
  53.7 0.0 copy-done.3
  53.7 2.7 %shard_map.77 = (bf16[256,768]{1,0:T(8,128)(2,1)S(1)}, bf16[768,768]{1,0:T(8,128)(2,1)}, f32[1,256]{1,0:T(1,128)}) custom-call(s32[1]{0:T(128)} %bitcast.side_ref, bf16[272,768]{1,0:T(8,128)(2,1)S(1)} %get-tuple-element.29.parcel_ref.own_ref, bf16[256,768]{1,0:T(8,128)(2,1)S(1)} %collective-permute-done.2.far_ref, ...), custom_call_target="tpu_custom_call" | custom-call | flops 503316480 | bytes 4352004 | tf_op jit(solution)/shard_map/pallas_call | solution.py:42
  56.3 1.8 %collective-permute-done.5.behind_ref = bf16[272,768]{1,0:T(8,128)(2,1)S(1)} collective-permute-done((bf16[272,768]{1,0:T(8,128)(2,1)S(1)}, bf16[272,768]{1,0:T(8,128)(2,1)S(1)}, u32[]{:S(2)}, u32[]{:S(2)}) %collective-permute-start.5) | collective-permute-done | bytes 417824 | tf_op jit(solution)/shard_map/ppermute | solution.py:24
  58.2 1.0 collective-permute-done.4.ahead_ref
  59.2 0.0 copy-start.6
  59.2 5.0 %all-to-all-start = ((bf16[16,48,768]{2,1,0:T(8,128)(2,1)}), bf16[16,48,768]{2,1,0:T(8,128)(2,1)}, u32[]{:S(2)}, u32[]{:S(2)}) async-start(bf16[16,48,768]{2,1,0:T(8,128)(2,1)} %bitcast.4), calls=%async_computation | async-start | bytes 2359296 | tf_op jit(solution)/shard_map/all_to_all | solution.py:177
  64.2 0.0 copy-done.6
  64.2 3.2 %shard_map.78 = (f32[256,768]{1,0:T(8,128)S(1)}, bf16[256,768]{1,0:T(8,128)(2,1)}) custom-call(s32[1]{0:T(128)} %bitcast.side_ref, bf16[256,768]{1,0:T(8,128)(2,1)S(1)} %copy-done.6, bf16[256,768]{1,0:T(8,128)(2,1)} %collective-permute-done.3.mate_ref, bf16[272,768]{1,0:T(8,128)(2,1)S(1)} %get-tuple-element.29.parcel_ref.own_ref, ...), custom_call_target="tpu_custom_call" | custom-call | flops 1006632960 | bytes 3219460 | tf_op jit(solution)/shard_map/pallas_call | solution.py:42
  67.4 0.0 copy-start.1
  67.5 2.3 %collective-permute-start.6 = (bf16[256,768]{1,0:T(8,128)(2,1)}, bf16[256,768]{1,0:T(8,128)(2,1)S(1)}, u32[]{:S(2)}, u32[]{:S(2)}) collective-permute-start(bf16[256,768]{1,0:T(8,128)(2,1)} %get-tuple-element.31), channel_id=1, source_target_pairs={{0,1},{1,0},{2,3},{3,2},{4,5},{5,4},{6,7},{7,6},{8,9},{9,8},{10,11... | collective-permute-start | bytes 1179656 | tf_op jit(solution)/shard_map/ppermute | solution.py:28
  69.8 13.3 %all-to-all-done = bf16[16,48,768]{2,1,0:T(8,128)(2,1)} async-done(((bf16[16,48,768]{2,1,0:T(8,128)(2,1)}), bf16[16,48,768]{2,1,0:T(8,128)(2,1)}, u32[]{:S(2)}, u32[]{:S(2)}) %all-to-all-start) | async-done | bytes 1179680 | tf_op jit(solution)/shard_map/all_to_all | solution.py:177
  83.0 1.6 %fusion = bf16[768,48]{0,1:T(8,128)(2,1)S(1)} fusion(bf16[16,48,768]{2,1,0:T(8,128)(2,1)} %all-to-all-done, bf16[48,48]{0,1:T(8,128)(2,1)S(1)} %fusion.2), kind=kOutput, calls=%fused_computation.2 | convolution fusion | flops 56659968 | bytes 1257984 | tf_op jit(solution)/shard_map/dot_general | solution.py:36
  84.7 0.2 copy.8
  84.8 0.9 reshape.46
  85.8 25.0 %all-to-all-start.1 = ((bf16[64,2,288]{2,1,0:T(2,128)(2,1)}), bf16[64,2,288]{2,1,0:T(2,128)(2,1)S(1)}, u32[]{:S(2)}, u32[]{:S(2)}) async-start(bf16[64,2,288]{2,1,0:T(2,128)(2,1)} %reshape.46), calls=%async_computation.1 | async-start | bytes 196608 | tf_op jit(solution)/shard_map/all_to_all | solution.py:192
  110.8 0.0 copy-done.1
  110.8 1.3 %convolution_convert_fusion = bf16[256,768]{1,0:T(8,128)(2,1)} fusion(bf16[256,768]{1,0:T(8,128)(2,1)S(1)} %get-tuple-element.27, bf16[768,768]{1,0:T(8,128)(2,1)S(1)} %copy-done.1), kind=kOutput, calls=%fused_computation | convolution fusion | flops 302186496 | bytes 1966080 | tf_op jit(solution)/shard_map/dot_general | solution.py:36
  112.0 0.0 collective-permute-done.6
  112.1 1.0 add_multiply_fusion
  113.0 7.7 %all-to-all-done.1 = bf16[64,2,288]{2,1,0:T(2,128)(2,1)S(1)} async-done(((bf16[64,2,288]{2,1,0:T(2,128)(2,1)}), bf16[64,2,288]{2,1,0:T(2,128)(2,1)S(1)}, u32[]{:S(2)}, u32[]{:S(2)}) %all-to-all-start.1) | async-done | bytes 73760 | tf_op jit(solution)/shard_map/all_to_all | solution.py:192
  120.7 0.1 convert_reduce_fusion
  120.9 0.7 reshape.47
  (1 shorter events, 0.0 us)
Async XLA Ops:
  0.6 32.9 %collective-permute-start.1 = (bf16[256,768]{1,0:T(8,128)(2,1)}, bf16[256,768]{1,0:T(8,128)(2,1)S(1)}, u32[]{:S(2)}, u32[]{:S(2)}) collective-permute-start(bf16[256,768]{1,0:T(8,128)(2,1)} %text_ref), channel_id=1, source_target_pairs={{1022,0},{1023,1},{0,2},{1,3},{2,4},{3,5},{4,6},{5,7},{6,8},{7,9},... | collective-permute-start | bytes 1179656 | tf_op jit(solution)/shard_map/ppermute | solution.py:24
  4.7 29.8 %collective-permute-start = (bf16[256,768]{1,0:T(8,128)(2,1)}, bf16[256,768]{1,0:T(8,128)(2,1)S(1)}, u32[]{:S(2)}, u32[]{:S(2)}) collective-permute-start(bf16[256,768]{1,0:T(8,128)(2,1)} %text_ref), channel_id=1, source_target_pairs={{2,0},{3,1},{4,2},{5,3},{6,4},{7,5},{8,6},{9,7},{10,8},{11,9},{12,... | collective-permute-start | bytes 1179656 | tf_op jit(solution)/shard_map/ppermute | solution.py:24
  26.4 23.7 %collective-permute-start.3 = (bf16[256,768]{1,0:T(8,128)(2,1)}, bf16[256,768]{1,0:T(8,128)(2,1)}, u32[]{:S(2)}, u32[]{:S(2)}) collective-permute-start(bf16[256,768]{1,0:T(8,128)(2,1)} %text_ref), channel_id=1, source_target_pairs={{0,1},{1,0},{2,3},{3,2},{4,5},{5,4},{6,7},{7,6},{8,9},{9,8},{10,11... | collective-permute-start | bytes 1179656 | tf_op jit(solution)/shard_map/ppermute | solution.py:28
  29.3 1.3 %copy-start = (bf16[768,768]{1,0:T(8,128)(2,1)S(1)}, bf16[768,768]{1,0:T(8,128)(2,1)}, u32[]{:S(2)}) copy-start(bf16[768,768]{1,0:T(8,128)(2,1)} %refs_2_.1) | copy-start | bytes 3538948
  30.6 1.0 copy-start.2
  31.6 0.7 copy-start.4
  32.3 17.9 %copy-start.5 = (bf16[256,768]{1,0:T(8,128)(2,1)S(1)}, bf16[256,768]{1,0:T(8,128)(2,1)}, u32[]{:S(2)}) copy-start(bf16[256,768]{1,0:T(8,128)(2,1)} %text_ref) | copy-start | bytes 1179652
  35.3 18.3 %collective-permute-start.2 = (bf16[256,768]{1,0:T(8,128)(2,1)}, bf16[256,768]{1,0:T(8,128)(2,1)S(1)}, u32[]{:S(2)}, u32[]{:S(2)}) collective-permute-start(bf16[256,768]{1,0:T(8,128)(2,1)} %broadcast_select_fusion), channel_id=1, source_target_pairs={{0,1},{1,0},{2,3},{3,2},{4,5},{5,4},{6,7},{7,6},{8,9},{9,8},{10,11... | collective-permute-start | bytes 1179656 | tf_op jit(solution)/shard_map/ppermute | solution.py:28
  38.8 19.4 %collective-permute-start.5 = (bf16[272,768]{1,0:T(8,128)(2,1)S(1)}, bf16[272,768]{1,0:T(8,128)(2,1)S(1)}, u32[]{:S(2)}, u32[]{:S(2)}) collective-permute-start(bf16[272,768]{1,0:T(8,128)(2,1)S(1)} %get-tuple-element.29.parcel_ref.own_ref), channel_id=1, source_target_pairs={{1022,0},{1023,1},{0,2},{1,3},{2,4},{3,5},{4,6},{5,7},{6,8},{7,9},... | collective-permute-start | bytes 1253384 | tf_op jit(solution)/shard_map/ppermute | solution.py:24
  40.7 18.5 %collective-permute-start.4 = (bf16[272,768]{1,0:T(8,128)(2,1)S(1)}, bf16[272,768]{1,0:T(8,128)(2,1)}, u32[]{:S(2)}, u32[]{:S(2)}) collective-permute-start(bf16[272,768]{1,0:T(8,128)(2,1)S(1)} %get-tuple-element.29.parcel_ref.own_ref), channel_id=1, source_target_pairs={{2,0},{3,1},{4,2},{5,3},{6,4},{7,5},{8,6},{9,7},{10,8},{11,9},{12,... | collective-permute-start | bytes 1253384 | tf_op jit(solution)/shard_map/ppermute | solution.py:24
  50.2 3.5 %copy-start.3 = (bf16[256,768]{1,0:T(8,128)(2,1)S(1)}, bf16[256,768]{1,0:T(8,128)(2,1)}, u32[]{:S(2)}) copy-start(bf16[256,768]{1,0:T(8,128)(2,1)} %feats_ref.1) | copy-start | bytes 1179652
  59.2 5.1 %copy-start.6 = (bf16[256,768]{1,0:T(8,128)(2,1)S(1)}, bf16[256,768]{1,0:T(8,128)(2,1)}, u32[]{:S(2)}) copy-start(bf16[256,768]{1,0:T(8,128)(2,1)} %text_ref) | copy-start | bytes 1179652
  59.2 23.9 %all-to-all-start = ((bf16[16,48,768]{2,1,0:T(8,128)(2,1)}), bf16[16,48,768]{2,1,0:T(8,128)(2,1)}, u32[]{:S(2)}, u32[]{:S(2)}) async-start(bf16[16,48,768]{2,1,0:T(8,128)(2,1)} %bitcast.4), calls=%async_computation | async-start | bytes 2359296 | tf_op jit(solution)/shard_map/all_to_all | solution.py:177
  67.4 43.3 %copy-start.1 = (bf16[768,768]{1,0:T(8,128)(2,1)S(1)}, bf16[768,768]{1,0:T(8,128)(2,1)}, u32[]{:S(2)}) copy-start(bf16[768,768]{1,0:T(8,128)(2,1)} %refs_2_.1) | copy-start | bytes 3538948
  67.5 44.6 %collective-permute-start.6 = (bf16[256,768]{1,0:T(8,128)(2,1)}, bf16[256,768]{1,0:T(8,128)(2,1)S(1)}, u32[]{:S(2)}, u32[]{:S(2)}) collective-permute-start(bf16[256,768]{1,0:T(8,128)(2,1)} %get-tuple-element.31), channel_id=1, source_target_pairs={{0,1},{1,0},{2,3},{3,2},{4,5},{5,4},{6,7},{7,6},{8,9},{9,8},{10,11... | collective-permute-start | bytes 1179656 | tf_op jit(solution)/shard_map/ppermute | solution.py:28
  85.8 35.0 %all-to-all-start.1 = ((bf16[64,2,288]{2,1,0:T(2,128)(2,1)}), bf16[64,2,288]{2,1,0:T(2,128)(2,1)S(1)}, u32[]{:S(2)}, u32[]{:S(2)}) async-start(bf16[64,2,288]{2,1,0:T(2,128)(2,1)} %reshape.46), calls=%async_computation.1 | async-start | bytes 196608 | tf_op jit(solution)/shard_map/all_to_all | solution.py:192

commit v5 on v4

--- a/solution.py
+++ b/solution.py
@@ -154,8 +154,6 @@
     ahead, behind, parcel = lax.optimization_barrier((ahead, behind, parcel))
     near = jnp.where(core == 0, ahead, behind)
     far = other_core(near)
-    sent = after(parcel, near)
-    parcel_ahead, parcel_behind = from_ahead(sent, HALF), from_ahead(sent, -HALF)
     grad, loss = kernel_call(
         image_start,
         [shape((rows, width), F32), shape((1, rows), F32)],
@@ -170,28 +168,30 @@
         2 * pair + product,
         1,
     )
-    terms = after(terms, parcel_ahead, parcel_behind)
-
     n_col, n_row = lax.axis_size(COL), lax.axis_size(ROW)
     cols, tall = width // n_col, width // n_row
     mine = lax.all_to_all(terms.reshape(n_col, cols, width), COL, 0, 0, tiled=True)
 
-    text_part, mate_part = kernel_call(
-        text_side,
-        [shape((rows, width), F32), shape((rows, width), BF16)],
-        [side, after(text_emb, proj_grad), mate, parcel, parcel_ahead, parcel_behind],
-        10 * pair,
-        1,
-    )
-    text_grad = TEMP * (text_part + other_core(mate_part).astype(F32))
     feat_grad = dot(proj_grad, head_weight, ((1,), (1,))).astype(BF16)
 
     pick = jnp.tile(jnp.eye(cols, dtype=BF16), (n_col, 1))
+    pick = after(pick, feat_grad)
     summed = dot(mine.reshape(width, width), pick, ((0,), (0,))).astype(BF16)
     order = [(i + n_row // 2) % n_row for i in range(n_row)]
     last = lax.all_to_all(
         summed.reshape(n_row, 2, tall * cols // 2), ROW, 0, 0, axis_index_groups=[order], tiled=True
     )
+    sent = after(parcel, summed)
+    parcel_ahead, parcel_behind = from_ahead(sent, HALF), from_ahead(sent, -HALF)
+    text_part, mate_part = kernel_call(
+        text_side,
+        [shape((rows, width), F32), shape((rows, width), BF16)],
+        [side, text_emb, mate, parcel, parcel_ahead, parcel_behind],
+        10 * pair,
+        1,
+    )
+    text_grad = TEMP * (text_part + other_core(mate_part).astype(F32))
+
     head_grad = jnp.sum(last.astype(F32), axis=0).reshape(tall, cols)
     return row_loss.reshape(rows), feat_grad, text_grad, head_grad
 

time: 122 us -> 119 us (0.975)
  the two profiles are of different devices: /device:TPU:1 before, /device:TPU:24 now
where the time goes in v5:
time: 119 us; the launch traced here: 118 us
  starting transfers between devices  75 us (63%)
  waiting for transfers between devices  25 us (21%)
  Pallas kernels  7.82 us (7%)
  local copies, waits for them, and re-layouts  4.75 us (4%)
  matrix products  2.91 us (2%)
  other arithmetic  1.88 us (2%)
    all_to_all x1, starting transfers between devices, local(): lax.all_to_all(terms.reshape(n_col, cols, width), COL, 0, 0, tiled=True)  28.1 us
    all_to_all x1, starting transfers between devices, local(): lax.all_to_all(summed.reshape(n_row, 2, tall * cols // 2), ROW, 0, 0, axi...  22.3 us
    ppermute x4, starting transfers between devices, from_ahead(): lax.ppermute(block, LOOP, [((i + distance) % n, i) for i in range(n)])  18.9 us
    all_to_all x1, waiting for transfers between devices, local(): lax.all_to_all(terms.reshape(n_col, cols, width), COL, 0, 0, tiled=True)  16.7 us
    pallas_call x4, Pallas kernels, kernel_call(): pl.pallas_call(body, out_shape=outs, in_specs=[SMEM] * scalars + [VMEM] *...  7.82 us
    ppermute x3, starting transfers between devices, other_core(): return lax.ppermute(block, CORE, [(0, 1), (1, 0)])  5.75 us
    all_to_all x1, waiting for transfers between devices, local(): lax.all_to_all(summed.reshape(n_row, 2, tall * cols // 2), ROW, 0, 0, axi...  5.31 us
    unnamed x12, local copies, waits for them, and re-layouts  2.95 us
  transfers between devices with their start and end apart: 9, of which 4 were waited for; matrix products, arithmetic and copies ran while one was open for 3% of the time, Pallas kernels for 4%

profile of v5, /device:TPU:24, one launch (start us, length us, event | category | flops | bytes accessed | tf_op | source)
XLA Modules:
  0.0 118.2 jit_solution(12785176375679368952)
XLA Ops:
  0.6 2.7 %collective-permute-start = (bf16[256,768]{1,0:T(8,128)(2,1)}, bf16[256,768]{1,0:T(8,128)(2,1)S(1)}, u32[]{:S(2)}, u32[]{:S(2)}) collective-permute-start(bf16[256,768]{1,0:T(8,128)(2,1)} %text_ref.1), channel_id=1, source_target_pairs={{2,0},{3,1},{4,2},{5,3},{6,4},{7,5},{8,6},{9,7},{10,8},{11,9},{12,... | collective-permute-start | bytes 1179656 | tf_op jit(solution)/shard_map/ppermute | solution.py:24
  3.3 6.8 %collective-permute-start.1 = (bf16[256,768]{1,0:T(8,128)(2,1)}, bf16[256,768]{1,0:T(8,128)(2,1)S(1)}, u32[]{:S(2)}, u32[]{:S(2)}) collective-permute-start(bf16[256,768]{1,0:T(8,128)(2,1)} %text_ref.1), channel_id=1, source_target_pairs={{1022,0},{1023,1},{0,2},{1,3},{2,4},{3,5},{4,6},{5,7},{6,8},{7,9},... | collective-permute-start | bytes 1179656 | tf_op jit(solution)/shard_map/ppermute | solution.py:24
  10.1 1.9 %collective-permute-start.3 = (bf16[256,768]{1,0:T(8,128)(2,1)}, bf16[256,768]{1,0:T(8,128)(2,1)S(1)}, u32[]{:S(2)}, u32[]{:S(2)}) collective-permute-start(bf16[256,768]{1,0:T(8,128)(2,1)} %text_ref.1), channel_id=1, source_target_pairs={{0,1},{1,0},{2,3},{3,2},{4,5},{5,4},{6,7},{7,6},{8,9},{9,8},{10,11... | collective-permute-start | bytes 1179656 | tf_op jit(solution)/shard_map/ppermute | solution.py:28
  12.0 0.0 copy-start
  12.1 1.3 %copy-done = bf16[768,768]{1,0:T(8,128)(2,1)S(1)} copy-done((bf16[768,768]{1,0:T(8,128)(2,1)S(1)}, bf16[768,768]{1,0:T(8,128)(2,1)}, u32[]{:S(2)}) %copy-start) | copy-done | bytes 1179672
  13.3 0.0 copy-start.2
  13.3 1.0 copy-done.2
  14.3 0.0 copy-start.4
  14.3 0.7 copy-done.4
  15.0 0.0 copy-start.5
  15.0 0.6 shard_map.75
  15.6 1.6 %collective-permute-done.ahead_ref = bf16[256,768]{1,0:T(8,128)(2,1)S(1)} collective-permute-done((bf16[256,768]{1,0:T(8,128)(2,1)}, bf16[256,768]{1,0:T(8,128)(2,1)S(1)}, u32[]{:S(2)}, u32[]{:S(2)}) %collective-permute-start) | collective-permute-done | bytes 393248 | tf_op jit(solution)/shard_map/ppermute | solution.py:24
  17.2 1.3 %collective-permute-done.1.behind_ref = bf16[256,768]{1,0:T(8,128)(2,1)S(1)} collective-permute-done((bf16[256,768]{1,0:T(8,128)(2,1)}, bf16[256,768]{1,0:T(8,128)(2,1)S(1)}, u32[]{:S(2)}, u32[]{:S(2)}) %collective-permute-start.1) | collective-permute-done | bytes 393248 | tf_op jit(solution)/shard_map/ppermute | solution.py:24
  18.5 0.8 broadcast_select_fusion
  19.3 1.9 %collective-permute-start.2 = (bf16[256,768]{1,0:T(8,128)(2,1)}, bf16[256,768]{1,0:T(8,128)(2,1)S(1)}, u32[]{:S(2)}, u32[]{:S(2)}) collective-permute-start(bf16[256,768]{1,0:T(8,128)(2,1)} %broadcast_select_fusion), channel_id=1, source_target_pairs={{0,1},{1,0},{2,3},{3,2},{4,5},{5,4},{6,7},{7,6},{8,9},{9,8},{10,11... | collective-permute-start | bytes 1179656 | tf_op jit(solution)/shard_map/ppermute | solution.py:28
  21.2 0.0 collective-permute-done.3.mate_ref
  21.2 0.0 copy-done.5
  21.2 0.0 copy-start.3
  21.2 2.4 %shard_map.76 = (f32[256,768]{1,0:T(8,128)S(1)}, f32[1,256]{1,0:T(1,128)S(1)}) custom-call(s32[1]{0:T(128)} %bitcast.side_ref, bf16[272,768]{1,0:T(8,128)(2,1)S(1)} %get-tuple-element.29.parcel_ref.own_ref, bf16[256,768]{1,0:T(8,128)(2,1)S(1)} %copy-done.5, bf16[256,768]{1,0:T(8,128)(2,1)S(1)} %collective-permute-done.3.mate_ref, ...), custom_call_target="tpu_custom_call" | custom-call | flops 805306368 | bytes 2778116 | tf_op jit(solution)/shard_map/pallas_call | solution.py:42
  23.7 0.0 collective-permute-done.2.far_ref
  23.7 0.0 copy-done.3
  23.7 2.7 %shard_map.77 = (bf16[256,768]{1,0:T(8,128)(2,1)S(1)}, bf16[768,768]{1,0:T(8,128)(2,1)}, f32[1,256]{1,0:T(1,128)}) custom-call(s32[1]{0:T(128)} %bitcast.side_ref, bf16[272,768]{1,0:T(8,128)(2,1)S(1)} %get-tuple-element.29.parcel_ref.own_ref, bf16[256,768]{1,0:T(8,128)(2,1)S(1)} %collective-permute-done.2.far_ref, ...), custom_call_target="tpu_custom_call" | custom-call | flops 503316480 | bytes 4352004 | tf_op jit(solution)/shard_map/pallas_call | solution.py:42
  26.4 0.0 copy-start.1
  26.4 28.1 %all-to-all-start = ((bf16[16,48,768]{2,1,0:T(8,128)(2,1)}), bf16[16,48,768]{2,1,0:T(8,128)(2,1)}, u32[]{:S(2)}, u32[]{:S(2)}) async-start(bf16[16,48,768]{2,1,0:T(8,128)(2,1)} %bitcast.4), calls=%async_computation | async-start | bytes 2359296 | tf_op jit(solution)/shard_map/all_to_all | solution.py:173
  54.5 0.0 copy-done.1
  54.5 1.3 %convolution_convert_fusion = bf16[256,768]{1,0:T(8,128)(2,1)} fusion(bf16[256,768]{1,0:T(8,128)(2,1)S(1)} %get-tuple-element.26, bf16[768,768]{1,0:T(8,128)(2,1)S(1)} %copy-done.1), kind=kOutput, calls=%fused_computation | convolution fusion | flops 302186496 | bytes 1966080 | tf_op jit(solution)/shard_map/dot_general | solution.py:36
  55.8 16.7 %all-to-all-done = bf16[16,48,768]{2,1,0:T(8,128)(2,1)} async-done(((bf16[16,48,768]{2,1,0:T(8,128)(2,1)}), bf16[16,48,768]{2,1,0:T(8,128)(2,1)}, u32[]{:S(2)}, u32[]{:S(2)}) %all-to-all-start) | async-done | bytes 1179680 | tf_op jit(solution)/shard_map/all_to_all | solution.py:173
  72.6 1.6 %convolution_convert_fusion.1 = bf16[768,48]{0,1:T(8,128)(2,1)S(1)} fusion(bf16[768,768]{1,0:T(8,128)(2,1)} %bitcast.5, bf16[768,48]{1,0:T(8,128)(2,1)S(1)} %bitcast.12), kind=kOutput, calls=%fused_computation.1 | convolution fusion | flops 56659968 | bytes 1327104 | tf_op jit(solution)/shard_map/dot_general | solution.py:36
  74.2 1.9 %collective-permute-start.4 = (bf16[272,768]{1,0:T(8,128)(2,1)S(1)}, bf16[272,768]{1,0:T(8,128)(2,1)S(1)}, u32[]{:S(2)}, u32[]{:S(2)}) collective-permute-start(bf16[272,768]{1,0:T(8,128)(2,1)S(1)} %get-tuple-element.29.parcel_ref.own_ref), channel_id=1, source_target_pairs={{2,0},{3,1},{4,2},{5,3},{6,4},{7,5},{8,6},{9,7},{10,8},{11,9},{12,... | collective-permute-start | bytes 1253384 | tf_op jit(solution)/shard_map/ppermute | solution.py:24
  76.1 7.5 %collective-permute-start.5 = (bf16[272,768]{1,0:T(8,128)(2,1)S(1)}, bf16[272,768]{1,0:T(8,128)(2,1)S(1)}, u32[]{:S(2)}, u32[]{:S(2)}) collective-permute-start(bf16[272,768]{1,0:T(8,128)(2,1)S(1)} %get-tuple-element.29.parcel_ref.own_ref), channel_id=1, source_target_pairs={{1022,0},{1023,1},{0,2},{1,3},{2,4},{3,5},{4,6},{5,7},{6,8},{7,9},... | collective-permute-start | bytes 1253384 | tf_op jit(solution)/shard_map/ppermute | solution.py:24
  83.7 0.2 copy.8
  83.9 0.9 reshape.49
  84.8 22.3 %all-to-all-start.1 = ((bf16[64,2,288]{2,1,0:T(2,128)(2,1)}), bf16[64,2,288]{2,1,0:T(2,128)(2,1)S(1)}, u32[]{:S(2)}, u32[]{:S(2)}) async-start(bf16[64,2,288]{2,1,0:T(2,128)(2,1)} %reshape.49), calls=%async_computation.1 | async-start | bytes 196608 | tf_op jit(solution)/shard_map/all_to_all | solution.py:181
  107.1 0.0 collective-permute-done.4.ahead_ref
  107.1 0.0 collective-permute-done.5.behind_ref
  107.1 2.1 %shard_map.78 = (f32[256,768]{1,0:T(8,128)S(1)}, bf16[256,768]{1,0:T(8,128)(2,1)S(1)}) custom-call(s32[1]{0:T(128)} %bitcast.side_ref, bf16[256,768]{1,0:T(8,128)(2,1)S(1)} %copy-done.5, bf16[256,768]{1,0:T(8,128)(2,1)S(1)} %collective-permute-done.3.mate_ref, bf16[272,768]{1,0:T(8,128)(2,1)S(1)} %get-tuple-element.29.parcel_ref.own_ref, ...), custom_call_target="tpu_custom_call" | custom-call | flops 1006632960 | bytes 3219460 | tf_op jit(solution)/shard_map/pallas_call | solution.py:42
  109.2 1.9 %collective-permute-start.6 = (bf16[256,768]{1,0:T(8,128)(2,1)S(1)}, bf16[256,768]{1,0:T(8,128)(2,1)S(1)}, u32[]{:S(2)}, u32[]{:S(2)}) collective-permute-start(bf16[256,768]{1,0:T(8,128)(2,1)S(1)} %get-tuple-element.31), channel_id=1, source_target_pairs={{0,1},{1,0},{2,3},{3,2},{4,5},{5,4},{6,7},{7,6},{8,9},{9,8},{10,11... | collective-permute-start | bytes 1179656 | tf_op jit(solution)/shard_map/ppermute | solution.py:28
  111.1 5.3 %all-to-all-done.1 = bf16[64,2,288]{2,1,0:T(2,128)(2,1)S(1)} async-done(((bf16[64,2,288]{2,1,0:T(2,128)(2,1)}), bf16[64,2,288]{2,1,0:T(2,128)(2,1)S(1)}, u32[]{:S(2)}, u32[]{:S(2)}) %all-to-all-start.1) | async-done | bytes 73760 | tf_op jit(solution)/shard_map/all_to_all | solution.py:181
  116.4 0.1 convert_reduce_fusion
  116.5 0.7 reshape.50
  117.2 0.0 collective-permute-done.6
  117.2 1.0 add_multiply_fusion
  (2 shorter events, 0.0 us)
Async XLA Ops:
  0.6 16.6 %collective-permute-start = (bf16[256,768]{1,0:T(8,128)(2,1)}, bf16[256,768]{1,0:T(8,128)(2,1)S(1)}, u32[]{:S(2)}, u32[]{:S(2)}) collective-permute-start(bf16[256,768]{1,0:T(8,128)(2,1)} %text_ref.1), channel_id=1, source_target_pairs={{2,0},{3,1},{4,2},{5,3},{6,4},{7,5},{8,6},{9,7},{10,8},{11,9},{12,... | collective-permute-start | bytes 1179656 | tf_op jit(solution)/shard_map/ppermute | solution.py:24
  3.3 15.2 %collective-permute-start.1 = (bf16[256,768]{1,0:T(8,128)(2,1)}, bf16[256,768]{1,0:T(8,128)(2,1)S(1)}, u32[]{:S(2)}, u32[]{:S(2)}) collective-permute-start(bf16[256,768]{1,0:T(8,128)(2,1)} %text_ref.1), channel_id=1, source_target_pairs={{1022,0},{1023,1},{0,2},{1,3},{2,4},{3,5},{4,6},{5,7},{6,8},{7,9},... | collective-permute-start | bytes 1179656 | tf_op jit(solution)/shard_map/ppermute | solution.py:24
  10.1 11.1 %collective-permute-start.3 = (bf16[256,768]{1,0:T(8,128)(2,1)}, bf16[256,768]{1,0:T(8,128)(2,1)S(1)}, u32[]{:S(2)}, u32[]{:S(2)}) collective-permute-start(bf16[256,768]{1,0:T(8,128)(2,1)} %text_ref.1), channel_id=1, source_target_pairs={{0,1},{1,0},{2,3},{3,2},{4,5},{5,4},{6,7},{7,6},{8,9},{9,8},{10,11... | collective-permute-start | bytes 1179656 | tf_op jit(solution)/shard_map/ppermute | solution.py:28
  12.0 1.3 %copy-start = (bf16[768,768]{1,0:T(8,128)(2,1)S(1)}, bf16[768,768]{1,0:T(8,128)(2,1)}, u32[]{:S(2)}) copy-start(bf16[768,768]{1,0:T(8,128)(2,1)} %refs_2_.1) | copy-start | bytes 3538948
  13.3 1.0 copy-start.2
  14.3 0.7 copy-start.4
  15.0 6.2 %copy-start.5 = (bf16[256,768]{1,0:T(8,128)(2,1)S(1)}, bf16[256,768]{1,0:T(8,128)(2,1)}, u32[]{:S(2)}) copy-start(bf16[256,768]{1,0:T(8,128)(2,1)} %text_ref.1) | copy-start | bytes 1179652
  19.3 4.4 %collective-permute-start.2 = (bf16[256,768]{1,0:T(8,128)(2,1)}, bf16[256,768]{1,0:T(8,128)(2,1)S(1)}, u32[]{:S(2)}, u32[]{:S(2)}) collective-permute-start(bf16[256,768]{1,0:T(8,128)(2,1)} %broadcast_select_fusion), channel_id=1, source_target_pairs={{0,1},{1,0},{2,3},{3,2},{4,5},{5,4},{6,7},{7,6},{8,9},{9,8},{10,11... | collective-permute-start | bytes 1179656 | tf_op jit(solution)/shard_map/ppermute | solution.py:28
  21.2 2.5 %copy-start.3 = (bf16[256,768]{1,0:T(8,128)(2,1)S(1)}, bf16[256,768]{1,0:T(8,128)(2,1)}, u32[]{:S(2)}) copy-start(bf16[256,768]{1,0:T(8,128)(2,1)} %feats_ref.1) | copy-start | bytes 1179652
  26.4 28.1 %copy-start.1 = (bf16[768,768]{1,0:T(8,128)(2,1)S(1)}, bf16[768,768]{1,0:T(8,128)(2,1)}, u32[]{:S(2)}) copy-start(bf16[768,768]{1,0:T(8,128)(2,1)} %refs_2_.1) | copy-start | bytes 3538948
  26.4 46.2 %all-to-all-start = ((bf16[16,48,768]{2,1,0:T(8,128)(2,1)}), bf16[16,48,768]{2,1,0:T(8,128)(2,1)}, u32[]{:S(2)}, u32[]{:S(2)}) async-start(bf16[16,48,768]{2,1,0:T(8,128)(2,1)} %bitcast.4), calls=%async_computation | async-start | bytes 2359296 | tf_op jit(solution)/shard_map/all_to_all | solution.py:173
  74.2 32.9 %collective-permute-start.4 = (bf16[272,768]{1,0:T(8,128)(2,1)S(1)}, bf16[272,768]{1,0:T(8,128)(2,1)S(1)}, u32[]{:S(2)}, u32[]{:S(2)}) collective-permute-start(bf16[272,768]{1,0:T(8,128)(2,1)S(1)} %get-tuple-element.29.parcel_ref.own_ref), channel_id=1, source_target_pairs={{2,0},{3,1},{4,2},{5,3},{6,4},{7,5},{8,6},{9,7},{10,8},{11,9},{12,... | collective-permute-start | bytes 1253384 | tf_op jit(solution)/shard_map/ppermute | solution.py:24
  76.1 30.9 %collective-permute-start.5 = (bf16[272,768]{1,0:T(8,128)(2,1)S(1)}, bf16[272,768]{1,0:T(8,128)(2,1)S(1)}, u32[]{:S(2)}, u32[]{:S(2)}) collective-permute-start(bf16[272,768]{1,0:T(8,128)(2,1)S(1)} %get-tuple-element.29.parcel_ref.own_ref), channel_id=1, source_target_pairs={{1022,0},{1023,1},{0,2},{1,3},{2,4},{3,5},{4,6},{5,7},{6,8},{7,9},... | collective-permute-start | bytes 1253384 | tf_op jit(solution)/shard_map/ppermute | solution.py:24
  84.8 31.6 %all-to-all-start.1 = ((bf16[64,2,288]{2,1,0:T(2,128)(2,1)}), bf16[64,2,288]{2,1,0:T(2,128)(2,1)S(1)}, u32[]{:S(2)}, u32[]{:S(2)}) async-start(bf16[64,2,288]{2,1,0:T(2,128)(2,1)} %reshape.49), calls=%async_computation.1 | async-start | bytes 196608 | tf_op jit(solution)/shard_map/all_to_all | solution.py:181
  109.2 8.0 %collective-permute-start.6 = (bf16[256,768]{1,0:T(8,128)(2,1)S(1)}, bf16[256,768]{1,0:T(8,128)(2,1)S(1)}, u32[]{:S(2)}, u32[]{:S(2)}) collective-permute-start(bf16[256,768]{1,0:T(8,128)(2,1)S(1)} %get-tuple-element.31), channel_id=1, source_target_pairs={{0,1},{1,0},{2,3},{3,2},{4,5},{5,4},{6,7},{7,6},{8,9},{9,8},{10,11... | collective-permute-start | bytes 1179656 | tf_op jit(solution)/shard_map/ppermute | solution.py:28

commit v6 on v2

--- a/solution.py
+++ b/solution.py
@@ -183,7 +183,7 @@
     summed = dot(mine.reshape(width, width), pick, ((0,), (0,))).astype(BF16)
     order = [(i + n_row // 2) % n_row for i in range(n_row)]
     last = lax.all_to_all(
-        summed.reshape(n_row, 8, tall * cols // 8), ROW, 0, 0, axis_index_groups=[order], tiled=True
+        summed.reshape(n_row, 2, tall * cols // 2), ROW, 0, 0, axis_index_groups=[order], tiled=True
     )
     head_grad = jnp.sum(last.astype(F32), axis=0).reshape(tall, cols)
     return row_loss.reshape(rows), feat_grad, text_grad, head_grad

time: 114 us -> 111 us (0.974)
  waiting for transfers between devices: 14.3 us -> 11.1 us
    all_to_all x1, waiting for transfers between devices: 4.24 us -> 1 us  [local(): lax.all_to_all(summed.reshape(n_row, 2, tall * cols // 2), ROW, 0, 0, axi...]
  transfers between devices with their start and end apart: 10 -> 10, of which waited for: 5 -> 5; matrix products, arithmetic and copies ran while one was open for 3% -> 3% of each run, Pallas kernels for 5% -> 6%
where the time goes in v6:
time: 111 us; the launch traced here: 110 us
  starting transfers between devices  82.1 us (74%)
  waiting for transfers between devices  11.1 us (10%)
  Pallas kernels  8.79 us (8%)
  local copies, waits for them, and re-layouts  4.73 us (4%)
  matrix products  1.6 us (1%)
    ppermute x4, starting transfers between devices, from_ahead(): lax.ppermute(block, LOOP, [((i + distance) % n, i) for i in range(n)])  40.2 us
    all_to_all x1, starting transfers between devices, local(): lax.all_to_all(summed.reshape(n_row, 2, tall * cols // 2), ROW, 0, 0, axi...  25.7 us
    ppermute x4, starting transfers between devices, other_core(): return lax.ppermute(block, CORE, [(0, 1), (1, 0)])  12.6 us
    pallas_call x4, Pallas kernels, kernel_call(): pl.pallas_call(body, out_shape=outs, in_specs=[SMEM] * scalars + [VMEM] *...  8.79 us
    all_to_all x1, waiting for transfers between devices, local(): lax.all_to_all(terms.reshape(n_col, cols, width), COL, 0, 0, tiled=True)  8.31 us
    all_to_all x1, starting transfers between devices, local(): lax.all_to_all(terms.reshape(n_col, cols, width), COL, 0, 0, tiled=True)  3.6 us
    unnamed x14, local copies, waits for them, and re-layouts  2.96 us
  transfers between devices with their start and end apart: 10, of which 5 were waited for; matrix products, arithmetic and copies ran while one was open for 3% of the time, Pallas kernels for 6%

profile of v6, /device:TPU:1, one launch (start us, length us, event | category | flops | bytes accessed | tf_op | source)
XLA Modules:
  0.0 110.2 jit_solution(8486131747980733949)
XLA Ops:
  0.6 4.0 %collective-permute-start.1 = (bf16[256,768]{1,0:T(8,128)(2,1)}, bf16[256,768]{1,0:T(8,128)(2,1)S(1)}, u32[]{:S(2)}, u32[]{:S(2)}) collective-permute-start(bf16[256,768]{1,0:T(8,128)(2,1)} %text_ref.1), channel_id=1, source_target_pairs={{1022,0},{1023,1},{0,2},{1,3},{2,4},{3,5},{4,6},{5,7},{6,8},{7,9},... | collective-permute-start | bytes 1179656 | tf_op jit(solution)/shard_map/ppermute | solution.py:24
  4.7 21.8 %collective-permute-start = (bf16[256,768]{1,0:T(8,128)(2,1)}, bf16[256,768]{1,0:T(8,128)(2,1)S(1)}, u32[]{:S(2)}, u32[]{:S(2)}) collective-permute-start(bf16[256,768]{1,0:T(8,128)(2,1)} %text_ref.1), channel_id=1, source_target_pairs={{2,0},{3,1},{4,2},{5,3},{6,4},{7,5},{8,6},{9,7},{10,8},{11,9},{12,... | collective-permute-start | bytes 1179656 | tf_op jit(solution)/shard_map/ppermute | solution.py:24
  26.4 2.9 %collective-permute-start.3 = (bf16[256,768]{1,0:T(8,128)(2,1)}, bf16[256,768]{1,0:T(8,128)(2,1)S(1)}, u32[]{:S(2)}, u32[]{:S(2)}) collective-permute-start(bf16[256,768]{1,0:T(8,128)(2,1)} %text_ref.1), channel_id=1, source_target_pairs={{0,1},{1,0},{2,3},{3,2},{4,5},{5,4},{6,7},{7,6},{8,9},{9,8},{10,11... | collective-permute-start | bytes 1179656 | tf_op jit(solution)/shard_map/ppermute | solution.py:28
  29.3 0.0 copy-start
  29.3 1.3 %copy-done = bf16[768,768]{1,0:T(8,128)(2,1)S(1)} copy-done((bf16[768,768]{1,0:T(8,128)(2,1)S(1)}, bf16[768,768]{1,0:T(8,128)(2,1)}, u32[]{:S(2)}) %copy-start) | copy-done | bytes 1179672
  30.6 0.0 copy-start.2
  30.6 1.0 copy-done.2
  31.6 0.0 copy-start.4
  31.6 0.7 copy-done.4
  32.3 0.0 copy-start.5
  32.3 0.6 shard_map.75
  32.9 0.7 collective-permute-done.1.behind_ref
  33.5 1.0 collective-permute-done.ahead_ref
  34.5 0.8 broadcast_select_fusion.1
  35.3 3.4 %collective-permute-start.2 = (bf16[256,768]{1,0:T(8,128)(2,1)}, bf16[256,768]{1,0:T(8,128)(2,1)S(1)}, u32[]{:S(2)}, u32[]{:S(2)}) collective-permute-start(bf16[256,768]{1,0:T(8,128)(2,1)} %broadcast_select_fusion.1), channel_id=1, source_target_pairs={{0,1},{1,0},{2,3},{3,2},{4,5},{5,4},{6,7},{7,6},{8,9},{9,8},{10,11... | collective-permute-start | bytes 1179656 | tf_op jit(solution)/shard_map/ppermute | solution.py:28
  38.8 0.0 collective-permute-done.3.mate_ref
  38.8 0.0 copy-done.5
  38.8 0.0 copy-start.3
  38.8 2.4 %shard_map.76 = (f32[256,768]{1,0:T(8,128)S(1)}, f32[1,256]{1,0:T(1,128)S(1)}) custom-call(s32[1]{0:T(128)} %bitcast.side_ref, bf16[272,768]{1,0:T(8,128)(2,1)S(1)} %get-tuple-element.25.parcel_ref.own_ref, bf16[256,768]{1,0:T(8,128)(2,1)S(1)} %copy-done.5, bf16[256,768]{1,0:T(8,128)(2,1)S(1)} %collective-permute-done.3.mate_ref, ...), custom_call_target="tpu_custom_call" | custom-call | flops 805306368 | bytes 2778116 | tf_op jit(solution)/shard_map/pallas_call | solution.py:42
  41.2 0.0 collective-permute-done.2.far_ref
  41.2 0.0 copy-done.3
  41.3 2.7 %shard_map.77 = (bf16[256,768]{1,0:T(8,128)(2,1)S(1)}, bf16[768,768]{1,0:T(8,128)(2,1)}, f32[1,256]{1,0:T(1,128)}) custom-call(s32[1]{0:T(128)} %bitcast.side_ref, bf16[272,768]{1,0:T(8,128)(2,1)S(1)} %get-tuple-element.25.parcel_ref.own_ref, bf16[256,768]{1,0:T(8,128)(2,1)S(1)} %collective-permute-done.2.far_ref, ...), custom_call_target="tpu_custom_call" | custom-call | flops 503316480 | bytes 4352004 | tf_op jit(solution)/shard_map/pallas_call | solution.py:42
  44.0 3.6 %all-to-all-start = ((bf16[16,48,768]{2,1,0:T(8,128)(2,1)}), bf16[16,48,768]{2,1,0:T(8,128)(2,1)S(1)}, u32[]{:S(2)}, u32[]{:S(2)}) async-start(bf16[16,48,768]{2,1,0:T(8,128)(2,1)} %bitcast.4), calls=%async_computation | async-start | bytes 2359296 | tf_op jit(solution)/shard_map/all_to_all | solution.py:171
  47.6 3.2 %collective-permute-start.6 = (bf16[272,768]{1,0:T(8,128)(2,1)S(1)}, bf16[272,768]{1,0:T(8,128)(2,1)S(1)}, u32[]{:S(2)}, u32[]{:S(2)}) collective-permute-start(bf16[272,768]{1,0:T(8,128)(2,1)S(1)} %get-tuple-element.25.parcel_ref.own_ref), channel_id=1, source_target_pairs={{1022,0},{1023,1},{0,2},{1,3},{2,4},{3,5},{4,6},{5,7},{6,8},{7,9},... | collective-permute-start | bytes 1253384 | tf_op jit(solution)/shard_map/ppermute | solution.py:24
  50.8 11.2 %collective-permute-start.5 = (bf16[272,768]{1,0:T(8,128)(2,1)S(1)}, bf16[272,768]{1,0:T(8,128)(2,1)S(1)}, u32[]{:S(2)}, u32[]{:S(2)}) collective-permute-start(bf16[272,768]{1,0:T(8,128)(2,1)S(1)} %get-tuple-element.25.parcel_ref.own_ref), channel_id=1, source_target_pairs={{2,0},{3,1},{4,2},{5,3},{6,4},{7,5},{8,6},{9,7},{10,8},{11,9},{12,... | collective-permute-start | bytes 1253384 | tf_op jit(solution)/shard_map/ppermute | solution.py:24
  62.0 2.5 %collective-permute-start.4 = (bf16[272,768]{1,0:T(8,128)(2,1)S(1)}, bf16[272,768]{1,0:T(8,128)(2,1)S(1)}, u32[]{:S(2)}, u32[]{:S(2)}) collective-permute-start(bf16[272,768]{1,0:T(8,128)(2,1)S(1)} %get-tuple-element.25.parcel_ref.own_ref), channel_id=1, source_target_pairs={{0,1},{1,0},{2,3},{3,2},{4,5},{5,4},{6,7},{7,6},{8,9},{9,8},{10,11... | collective-permute-start | bytes 1253384 | tf_op jit(solution)/shard_map/ppermute | solution.py:28
  64.6 8.3 %all-to-all-done = bf16[16,48,768]{2,1,0:T(8,128)(2,1)S(1)} async-done(((bf16[16,48,768]{2,1,0:T(8,128)(2,1)}), bf16[16,48,768]{2,1,0:T(8,128)(2,1)S(1)}, u32[]{:S(2)}, u32[]{:S(2)}) %all-to-all-start) | async-done | bytes 1179680 | tf_op jit(solution)/shard_map/all_to_all | solution.py:171
  72.9 0.3 fusion
  73.3 0.0 copy-start.1
  73.3 0.2 copy.8
  73.4 0.9 reshape.46
  74.4 25.7 %all-to-all-start.1 = ((bf16[64,2,288]{2,1,0:T(2,128)(2,1)}), bf16[64,2,288]{2,1,0:T(2,128)(2,1)S(1)}, u32[]{:S(2)}, u32[]{:S(2)}) async-start(bf16[64,2,288]{2,1,0:T(2,128)(2,1)} %reshape.46), calls=%async_computation.1 | async-start | bytes 196608 | tf_op jit(solution)/shard_map/all_to_all | solution.py:185
  100.1 0.0 collective-permute-done.6.behind_ref
  100.1 0.0 collective-permute-done.5.ahead_ref
  100.1 0.1 broadcast_select_fusion
  100.2 0.0 copy-start.6
  100.2 3.8 %collective-permute-start.7 = (bf16[272,768]{1,0:T(8,128)(2,1)S(1)}, bf16[272,768]{1,0:T(8,128)(2,1)S(1)}, u32[]{:S(2)}, u32[]{:S(2)}) collective-permute-start(bf16[272,768]{1,0:T(8,128)(2,1)S(1)} %broadcast_select_fusion), channel_id=1, source_target_pairs={{0,1},{1,0},{2,3},{3,2},{4,5},{5,4},{6,7},{7,6},{8,9},{9,8},{10,11... | collective-permute-start | bytes 1253384 | tf_op jit(solution)/shard_map/ppermute | solution.py:28
  103.9 0.0 copy-done.1
  103.9 1.3 %convolution_convert_fusion = bf16[256,768]{1,0:T(8,128)(2,1)} fusion(bf16[256,768]{1,0:T(8,128)(2,1)S(1)} %get-tuple-element.23, bf16[768,768]{1,0:T(8,128)(2,1)S(1)} %copy-done.1), kind=kOutput, calls=%fused_computation | convolution fusion | flops 302186496 | bytes 1966080 | tf_op jit(solution)/shard_map/dot_general | solution.py:36
  105.2 0.0 collective-permute-done.4.mate_ref
  105.2 0.1 collective-permute-done.7.far_ref
  105.3 0.0 copy-done.6
  105.3 3.0 %shard_map.78 = f32[256,768]{1,0:T(8,128)} custom-call(s32[1]{0:T(128)} %bitcast.side_ref, bf16[256,768]{1,0:T(8,128)(2,1)S(1)} %copy-done.6, bf16[272,768]{1,0:T(8,128)(2,1)S(1)} %get-tuple-element.25.parcel_ref.own_ref, bf16[272,768]{1,0:T(8,128)(2,1)S(1)} %collective-permute-done.4.mate_ref, bf16[272,768]{1,0:T(8,128)(2,1)S(1)} %collective-permute-done.5.ahead_ref, ...), custom_call_target="tpu_custom_call" | custom-call | flops 1006632960 | bytes 3268612 | tf_op jit(solution)/shard_map/pallas_call | solution.py:42
  108.4 1.0 all-to-all-done.1
  109.4 0.1 convert_reduce_fusion
  109.5 0.7 reshape.47
  (1 shorter events, 0.0 us)
Async XLA Ops:
  0.6 32.9 %collective-permute-start.1 = (bf16[256,768]{1,0:T(8,128)(2,1)}, bf16[256,768]{1,0:T(8,128)(2,1)S(1)}, u32[]{:S(2)}, u32[]{:S(2)}) collective-permute-start(bf16[256,768]{1,0:T(8,128)(2,1)} %text_ref.1), channel_id=1, source_target_pairs={{1022,0},{1023,1},{0,2},{1,3},{2,4},{3,5},{4,6},{5,7},{6,8},{7,9},... | collective-permute-start | bytes 1179656 | tf_op jit(solution)/shard_map/ppermute | solution.py:24
  4.7 29.8 %collective-permute-start = (bf16[256,768]{1,0:T(8,128)(2,1)}, bf16[256,768]{1,0:T(8,128)(2,1)S(1)}, u32[]{:S(2)}, u32[]{:S(2)}) collective-permute-start(bf16[256,768]{1,0:T(8,128)(2,1)} %text_ref.1), channel_id=1, source_target_pairs={{2,0},{3,1},{4,2},{5,3},{6,4},{7,5},{8,6},{9,7},{10,8},{11,9},{12,... | collective-permute-start | bytes 1179656 | tf_op jit(solution)/shard_map/ppermute | solution.py:24
  26.4 12.3 %collective-permute-start.3 = (bf16[256,768]{1,0:T(8,128)(2,1)}, bf16[256,768]{1,0:T(8,128)(2,1)S(1)}, u32[]{:S(2)}, u32[]{:S(2)}) collective-permute-start(bf16[256,768]{1,0:T(8,128)(2,1)} %text_ref.1), channel_id=1, source_target_pairs={{0,1},{1,0},{2,3},{3,2},{4,5},{5,4},{6,7},{7,6},{8,9},{9,8},{10,11... | collective-permute-start | bytes 1179656 | tf_op jit(solution)/shard_map/ppermute | solution.py:28
  29.3 1.3 %copy-start = (bf16[768,768]{1,0:T(8,128)(2,1)S(1)}, bf16[768,768]{1,0:T(8,128)(2,1)}, u32[]{:S(2)}) copy-start(bf16[768,768]{1,0:T(8,128)(2,1)} %refs_2_.1) | copy-start | bytes 3538948
  30.6 1.0 copy-start.2
  31.6 0.7 copy-start.4
  32.3 6.5 %copy-start.5 = (bf16[256,768]{1,0:T(8,128)(2,1)S(1)}, bf16[256,768]{1,0:T(8,128)(2,1)}, u32[]{:S(2)}) copy-start(bf16[256,768]{1,0:T(8,128)(2,1)} %text_ref.1) | copy-start | bytes 1179652
  35.3 5.9 %collective-permute-start.2 = (bf16[256,768]{1,0:T(8,128)(2,1)}, bf16[256,768]{1,0:T(8,128)(2,1)S(1)}, u32[]{:S(2)}, u32[]{:S(2)}) collective-permute-start(bf16[256,768]{1,0:T(8,128)(2,1)} %broadcast_select_fusion.1), channel_id=1, source_target_pairs={{0,1},{1,0},{2,3},{3,2},{4,5},{5,4},{6,7},{7,6},{8,9},{9,8},{10,11... | collective-permute-start | bytes 1179656 | tf_op jit(solution)/shard_map/ppermute | solution.py:28
  38.8 2.5 %copy-start.3 = (bf16[256,768]{1,0:T(8,128)(2,1)S(1)}, bf16[256,768]{1,0:T(8,128)(2,1)}, u32[]{:S(2)}) copy-start(bf16[256,768]{1,0:T(8,128)(2,1)} %feats_ref.1) | copy-start | bytes 1179652
  44.0 28.9 %all-to-all-start = ((bf16[16,48,768]{2,1,0:T(8,128)(2,1)}), bf16[16,48,768]{2,1,0:T(8,128)(2,1)S(1)}, u32[]{:S(2)}, u32[]{:S(2)}) async-start(bf16[16,48,768]{2,1,0:T(8,128)(2,1)} %bitcast.4), calls=%async_computation | async-start | bytes 2359296 | tf_op jit(solution)/shard_map/all_to_all | solution.py:171
  47.6 52.5 %collective-permute-start.6 = (bf16[272,768]{1,0:T(8,128)(2,1)S(1)}, bf16[272,768]{1,0:T(8,128)(2,1)S(1)}, u32[]{:S(2)}, u32[]{:S(2)}) collective-permute-start(bf16[272,768]{1,0:T(8,128)(2,1)S(1)} %get-tuple-element.25.parcel_ref.own_ref), channel_id=1, source_target_pairs={{1022,0},{1023,1},{0,2},{1,3},{2,4},{3,5},{4,6},{5,7},{6,8},{7,9},... | collective-permute-start | bytes 1253384 | tf_op jit(solution)/shard_map/ppermute | solution.py:24
  50.8 49.3 %collective-permute-start.5 = (bf16[272,768]{1,0:T(8,128)(2,1)S(1)}, bf16[272,768]{1,0:T(8,128)(2,1)S(1)}, u32[]{:S(2)}, u32[]{:S(2)}) collective-permute-start(bf16[272,768]{1,0:T(8,128)(2,1)S(1)} %get-tuple-element.25.parcel_ref.own_ref), channel_id=1, source_target_pairs={{2,0},{3,1},{4,2},{5,3},{6,4},{7,5},{8,6},{9,7},{10,8},{11,9},{12,... | collective-permute-start | bytes 1253384 | tf_op jit(solution)/shard_map/ppermute | solution.py:24
  62.0 43.2 %collective-permute-start.4 = (bf16[272,768]{1,0:T(8,128)(2,1)S(1)}, bf16[272,768]{1,0:T(8,128)(2,1)S(1)}, u32[]{:S(2)}, u32[]{:S(2)}) collective-permute-start(bf16[272,768]{1,0:T(8,128)(2,1)S(1)} %get-tuple-element.25.parcel_ref.own_ref), channel_id=1, source_target_pairs={{0,1},{1,0},{2,3},{3,2},{4,5},{5,4},{6,7},{7,6},{8,9},{9,8},{10,11... | collective-permute-start | bytes 1253384 | tf_op jit(solution)/shard_map/ppermute | solution.py:28
  73.3 30.7 %copy-start.1 = (bf16[768,768]{1,0:T(8,128)(2,1)S(1)}, bf16[768,768]{1,0:T(8,128)(2,1)}, u32[]{:S(2)}) copy-start(bf16[768,768]{1,0:T(8,128)(2,1)} %refs_2_.1) | copy-start | bytes 3538948
  74.4 35.0 %all-to-all-start.1 = ((bf16[64,2,288]{2,1,0:T(2,128)(2,1)}), bf16[64,2,288]{2,1,0:T(2,128)(2,1)S(1)}, u32[]{:S(2)}, u32[]{:S(2)}) async-start(bf16[64,2,288]{2,1,0:T(2,128)(2,1)} %reshape.46), calls=%async_computation.1 | async-start | bytes 196608 | tf_op jit(solution)/shard_map/all_to_all | solution.py:185
  100.2 5.2 %copy-start.6 = (bf16[256,768]{1,0:T(8,128)(2,1)S(1)}, bf16[256,768]{1,0:T(8,128)(2,1)}, u32[]{:S(2)}) copy-start(bf16[256,768]{1,0:T(8,128)(2,1)} %text_ref.1) | copy-start | bytes 1179652
  100.2 5.1 %collective-permute-start.7 = (bf16[272,768]{1,0:T(8,128)(2,1)S(1)}, bf16[272,768]{1,0:T(8,128)(2,1)S(1)}, u32[]{:S(2)}, u32[]{:S(2)}) collective-permute-start(bf16[272,768]{1,0:T(8,128)(2,1)S(1)} %broadcast_select_fusion), channel_id=1, source_target_pairs={{0,1},{1,0},{2,3},{3,2},{4,5},{5,4},{6,7},{7,6},{8,9},{9,8},{10,11... | collective-permute-start | bytes 1253384 | tf_op jit(solution)/shard_map/ppermute | solution.py:28

commit v7 on v6

--- a/solution.py
+++ b/solution.py
@@ -180,6 +180,7 @@
     feat_grad = dot(proj_grad, head_weight, ((1,), (1,))).astype(BF16)
 
     pick = jnp.tile(jnp.eye(cols, dtype=BF16), (n_col, 1))
+    pick = after(pick, feat_grad)
     summed = dot(mine.reshape(width, width), pick, ((0,), (0,))).astype(BF16)
     order = [(i + n_row // 2) % n_row for i in range(n_row)]
     last = lax.all_to_all(

time: 111 us -> 116 us (1.045)
  waiting for transfers between devices: 11.1 us -> 26.2 us
  starting transfers between devices: 82.1 us -> 71.1 us
  matrix products: 1.6 us -> 2.9 us
    ppermute x4, starting transfers between devices: 40.2 us -> 31.4 us  [from_ahead(): lax.ppermute(block, LOOP, [((i + distance) % n, i) for i in range(n)])]
    all_to_all x1, waiting for transfers between devices: 8.31 us -> 15.8 us  [local(): lax.all_to_all(terms.reshape(n_col, cols, width), COL, 0, 0, tiled=True)]
    ppermute x4, waiting for transfers between devices: 1.65 us -> 8.84 us  [from_ahead(): lax.ppermute(block, LOOP, [((i + distance) % n, i) for i in range(n)])]
    all_to_all x1, starting transfers between devices: 25.7 us -> 21.7 us  [local(): lax.all_to_all(summed.reshape(n_row, 2, tall * cols // 2), ROW, 0, 0, axi...]
    dot_general x2, matrix products: 1.6 us -> 2.9 us  [dot(): return lax.dot_general(a, b, (dims, ((), ())), preferred_element_type=F32)]
    ppermute x4, waiting for transfers between devices: 0.1 us -> 1.36 us  [other_core(): return lax.ppermute(block, CORE, [(0, 1), (1, 0)])]
  transfers between devices with their start and end apart: 10 -> 10, of which waited for: 5 -> 4; matrix products, arithmetic and copies ran while one was open for 3% -> 4% of each run, Pallas kernels for 6% -> 5%
where the time goes in v7:
time: 116 us; the launch traced here: 115 us
  starting transfers between devices  71.1 us (61%)
  waiting for transfers between devices  26.2 us (23%)
  Pallas kernels  8.76 us (8%)
  local copies, waits for them, and re-layouts  4.75 us (4%)
  matrix products  2.9 us (2%)
    ppermute x4, starting transfers between devices, from_ahead(): lax.ppermute(block, LOOP, [((i + distance) % n, i) for i in range(n)])  31.4 us
    all_to_all x1, starting transfers between devices, local(): lax.all_to_all(summed.reshape(n_row, 2, tall * cols // 2), ROW, 0, 0, axi...  21.7 us
    all_to_all x1, waiting for transfers between devices, local(): lax.all_to_all(terms.reshape(n_col, cols, width), COL, 0, 0, tiled=True)  15.8 us
    ppermute x4, starting transfers between devices, other_core(): return lax.ppermute(block, CORE, [(0, 1), (1, 0)])  13.5 us
    ppermute x4, waiting for transfers between devices, from_ahead(): lax.ppermute(block, LOOP, [((i + distance) % n, i) for i in range(n)])  8.84 us
    pallas_call x4, Pallas kernels, kernel_call(): pl.pallas_call(body, out_shape=outs, in_specs=[SMEM] * scalars + [VMEM] *...  8.76 us
    all_to_all x1, starting transfers between devices, local(): lax.all_to_all(terms.reshape(n_col, cols, width), COL, 0, 0, tiled=True)  4.41 us
    unnamed x14, local copies, waits for them, and re-layouts  2.96 us
  transfers between devices with their start and end apart: 10, of which 4 were waited for; matrix products, arithmetic and copies ran while one was open for 4% of the time, Pallas kernels for 5%

profile of v7, /device:TPU:1, one launch (start us, length us, event | category | flops | bytes accessed | tf_op | source)
XLA Modules:
  0.0 115.5 jit_solution(1060564144035691616)
XLA Ops:
  0.6 23.9 %collective-permute-start = (bf16[256,768]{1,0:T(8,128)(2,1)}, bf16[256,768]{1,0:T(8,128)(2,1)S(1)}, u32[]{:S(2)}, u32[]{:S(2)}) collective-permute-start(bf16[256,768]{1,0:T(8,128)(2,1)} %text_ref.1), channel_id=1, source_target_pairs={{2,0},{3,1},{4,2},{5,3},{6,4},{7,5},{8,6},{9,7},{10,8},{11,9},{12,... | collective-permute-start | bytes 1179656 | tf_op jit(solution)/shard_map/ppermute | solution.py:24
  24.5 1.9 %collective-permute-start.1 = (bf16[256,768]{1,0:T(8,128)(2,1)}, bf16[256,768]{1,0:T(8,128)(2,1)S(1)}, u32[]{:S(2)}, u32[]{:S(2)}) collective-permute-start(bf16[256,768]{1,0:T(8,128)(2,1)} %text_ref.1), channel_id=1, source_target_pairs={{1022,0},{1023,1},{0,2},{1,3},{2,4},{3,5},{4,6},{5,7},{6,8},{7,9},... | collective-permute-start | bytes 1179656 | tf_op jit(solution)/shard_map/ppermute | solution.py:24
  26.4 2.9 %collective-permute-start.3 = (bf16[256,768]{1,0:T(8,128)(2,1)}, bf16[256,768]{1,0:T(8,128)(2,1)S(1)}, u32[]{:S(2)}, u32[]{:S(2)}) collective-permute-start(bf16[256,768]{1,0:T(8,128)(2,1)} %text_ref.1), channel_id=1, source_target_pairs={{0,1},{1,0},{2,3},{3,2},{4,5},{5,4},{6,7},{7,6},{8,9},{9,8},{10,11... | collective-permute-start | bytes 1179656 | tf_op jit(solution)/shard_map/ppermute | solution.py:28
  29.3 0.0 copy-start
  29.3 1.3 %copy-done = bf16[768,768]{1,0:T(8,128)(2,1)S(1)} copy-done((bf16[768,768]{1,0:T(8,128)(2,1)S(1)}, bf16[768,768]{1,0:T(8,128)(2,1)}, u32[]{:S(2)}) %copy-start) | copy-done | bytes 1179672
  30.6 0.0 copy-start.2
  30.6 1.0 copy-done.2
  31.6 0.0 copy-start.4
  31.6 0.7 copy-done.4
  32.3 0.0 copy-start.5
  32.3 0.6 shard_map.75
  32.9 0.0 collective-permute-done.ahead_ref
  32.9 8.8 %collective-permute-done.1.behind_ref = bf16[256,768]{1,0:T(8,128)(2,1)S(1)} collective-permute-done((bf16[256,768]{1,0:T(8,128)(2,1)}, bf16[256,768]{1,0:T(8,128)(2,1)S(1)}, u32[]{:S(2)}, u32[]{:S(2)}) %collective-permute-start.1) | collective-permute-done | bytes 393248 | tf_op jit(solution)/shard_map/ppermute | solution.py:24
  41.7 0.8 broadcast_select_fusion.1
  42.5 3.8 %collective-permute-start.2 = (bf16[256,768]{1,0:T(8,128)(2,1)}, bf16[256,768]{1,0:T(8,128)(2,1)S(1)}, u32[]{:S(2)}, u32[]{:S(2)}) collective-permute-start(bf16[256,768]{1,0:T(8,128)(2,1)} %broadcast_select_fusion.1), channel_id=1, source_target_pairs={{0,1},{1,0},{2,3},{3,2},{4,5},{5,4},{6,7},{7,6},{8,9},{9,8},{10,11... | collective-permute-start | bytes 1179656 | tf_op jit(solution)/shard_map/ppermute | solution.py:28
  46.3 0.0 collective-permute-done.3.mate_ref
  46.3 0.0 copy-done.5
  46.3 0.0 copy-start.3
  46.3 2.4 %shard_map.76 = (f32[256,768]{1,0:T(8,128)S(1)}, f32[1,256]{1,0:T(1,128)S(1)}) custom-call(s32[1]{0:T(128)} %bitcast.side_ref, bf16[272,768]{1,0:T(8,128)(2,1)S(1)} %get-tuple-element.26.parcel_ref.own_ref, bf16[256,768]{1,0:T(8,128)(2,1)S(1)} %copy-done.5, bf16[256,768]{1,0:T(8,128)(2,1)S(1)} %collective-permute-done.3.mate_ref, ...), custom_call_target="tpu_custom_call" | custom-call | flops 805306368 | bytes 2778116 | tf_op jit(solution)/shard_map/pallas_call | solution.py:42
  48.8 0.0 collective-permute-done.2.far_ref
  48.8 0.0 copy-done.3
  48.8 2.7 %shard_map.77 = (bf16[256,768]{1,0:T(8,128)(2,1)S(1)}, bf16[768,768]{1,0:T(8,128)(2,1)}, f32[1,256]{1,0:T(1,128)}) custom-call(s32[1]{0:T(128)} %bitcast.side_ref, bf16[272,768]{1,0:T(8,128)(2,1)S(1)} %get-tuple-element.26.parcel_ref.own_ref, bf16[256,768]{1,0:T(8,128)(2,1)S(1)} %collective-permute-done.2.far_ref, ...), custom_call_target="tpu_custom_call" | custom-call | flops 503316480 | bytes 4352004 | tf_op jit(solution)/shard_map/pallas_call | solution.py:42
  51.4 0.0 copy-start.1
  51.4 4.4 %all-to-all-start = ((bf16[16,48,768]{2,1,0:T(8,128)(2,1)}), bf16[16,48,768]{2,1,0:T(8,128)(2,1)}, u32[]{:S(2)}, u32[]{:S(2)}) async-start(bf16[16,48,768]{2,1,0:T(8,128)(2,1)} %bitcast.4), calls=%async_computation | async-start | bytes 2359296 | tf_op jit(solution)/shard_map/all_to_all | solution.py:171
  55.9 3.7 %collective-permute-start.5 = (bf16[272,768]{1,0:T(8,128)(2,1)S(1)}, bf16[272,768]{1,0:T(8,128)(2,1)S(1)}, u32[]{:S(2)}, u32[]{:S(2)}) collective-permute-start(bf16[272,768]{1,0:T(8,128)(2,1)S(1)} %get-tuple-element.26.parcel_ref.own_ref), channel_id=1, source_target_pairs={{2,0},{3,1},{4,2},{5,3},{6,4},{7,5},{8,6},{9,7},{10,8},{11,9},{12,... | collective-permute-start | bytes 1253384 | tf_op jit(solution)/shard_map/ppermute | solution.py:24
  59.6 1.9 %collective-permute-start.6 = (bf16[272,768]{1,0:T(8,128)(2,1)S(1)}, bf16[272,768]{1,0:T(8,128)(2,1)S(1)}, u32[]{:S(2)}, u32[]{:S(2)}) collective-permute-start(bf16[272,768]{1,0:T(8,128)(2,1)S(1)} %get-tuple-element.26.parcel_ref.own_ref), channel_id=1, source_target_pairs={{1022,0},{1023,1},{0,2},{1,3},{2,4},{3,5},{4,6},{5,7},{6,8},{7,9},... | collective-permute-start | bytes 1253384 | tf_op jit(solution)/shard_map/ppermute | solution.py:24
  61.5 2.5 %collective-permute-start.4 = (bf16[272,768]{1,0:T(8,128)(2,1)S(1)}, bf16[272,768]{1,0:T(8,128)(2,1)S(1)}, u32[]{:S(2)}, u32[]{:S(2)}) collective-permute-start(bf16[272,768]{1,0:T(8,128)(2,1)S(1)} %get-tuple-element.26.parcel_ref.own_ref), channel_id=1, source_target_pairs={{0,1},{1,0},{2,3},{3,2},{4,5},{5,4},{6,7},{7,6},{8,9},{9,8},{10,11... | collective-permute-start | bytes 1253384 | tf_op jit(solution)/shard_map/ppermute | solution.py:28
  64.0 0.0 copy-done.1
  64.1 1.3 %convolution_convert_fusion = bf16[256,768]{1,0:T(8,128)(2,1)} fusion(bf16[256,768]{1,0:T(8,128)(2,1)S(1)} %get-tuple-element.24, bf16[768,768]{1,0:T(8,128)(2,1)S(1)} %copy-done.1), kind=kOutput, calls=%fused_computation | convolution fusion | flops 302186496 | bytes 1966080 | tf_op jit(solution)/shard_map/dot_general | solution.py:36
  65.3 15.8 %all-to-all-done = bf16[16,48,768]{2,1,0:T(8,128)(2,1)} async-done(((bf16[16,48,768]{2,1,0:T(8,128)(2,1)}), bf16[16,48,768]{2,1,0:T(8,128)(2,1)}, u32[]{:S(2)}, u32[]{:S(2)}) %all-to-all-start) | async-done | bytes 1179680 | tf_op jit(solution)/shard_map/all_to_all | solution.py:171
  81.2 1.6 %convolution_convert_fusion.1 = bf16[768,48]{0,1:T(8,128)(2,1)S(1)} fusion(bf16[768,768]{1,0:T(8,128)(2,1)} %bitcast.5, bf16[768,48]{1,0:T(8,128)(2,1)S(1)} %bitcast.12), kind=kOutput, calls=%fused_computation.1 | convolution fusion | flops 56659968 | bytes 1327104 | tf_op jit(solution)/shard_map/dot_general | solution.py:36
  82.8 0.0 copy-start.6
  82.8 0.2 copy.8
  83.0 0.9 reshape.49
  83.9 21.7 %all-to-all-start.1 = ((bf16[64,2,288]{2,1,0:T(2,128)(2,1)}), bf16[64,2,288]{2,1,0:T(2,128)(2,1)S(1)}, u32[]{:S(2)}, u32[]{:S(2)}) async-start(bf16[64,2,288]{2,1,0:T(2,128)(2,1)} %reshape.49), calls=%async_computation.1 | async-start | bytes 196608 | tf_op jit(solution)/shard_map/all_to_all | solution.py:186
  105.7 0.0 collective-permute-done.5.ahead_ref
  105.7 0.0 collective-permute-done.6.behind_ref
  105.7 0.1 broadcast_select_fusion
  105.7 4.4 %collective-permute-start.7 = (bf16[272,768]{1,0:T(8,128)(2,1)S(1)}, bf16[272,768]{1,0:T(8,128)(2,1)S(1)}, u32[]{:S(2)}, u32[]{:S(2)}) collective-permute-start(bf16[272,768]{1,0:T(8,128)(2,1)S(1)} %broadcast_select_fusion), channel_id=1, source_target_pairs={{0,1},{1,0},{2,3},{3,2},{4,5},{5,4},{6,7},{7,6},{8,9},{9,8},{10,11... | collective-permute-start | bytes 1253384 | tf_op jit(solution)/shard_map/ppermute | solution.py:28
  110.1 0.0 collective-permute-done.4.mate_ref
  110.1 1.4 %collective-permute-done.7.far_ref = bf16[272,768]{1,0:T(8,128)(2,1)S(1)} collective-permute-done((bf16[272,768]{1,0:T(8,128)(2,1)S(1)}, bf16[272,768]{1,0:T(8,128)(2,1)S(1)}, u32[]{:S(2)}, u32[]{:S(2)}) %collective-permute-start.7) | collective-permute-done | bytes 417824 | tf_op jit(solution)/shard_map/ppermute | solution.py:28
  111.5 0.0 copy-done.6
  111.5 3.1 %shard_map.78 = f32[256,768]{1,0:T(8,128)} custom-call(s32[1]{0:T(128)} %bitcast.side_ref, bf16[256,768]{1,0:T(8,128)(2,1)S(1)} %copy-done.6, bf16[272,768]{1,0:T(8,128)(2,1)S(1)} %get-tuple-element.26.parcel_ref.own_ref, bf16[272,768]{1,0:T(8,128)(2,1)S(1)} %collective-permute-done.4.mate_ref, bf16[272,768]{1,0:T(8,128)(2,1)S(1)} %collective-permute-done.5.ahead_ref, ...), custom_call_target="tpu_custom_call" | custom-call | flops 1006632960 | bytes 3268612 | tf_op jit(solution)/shard_map/pallas_call | solution.py:42
  114.5 0.1 all-to-all-done.1
  114.7 0.1 convert_reduce_fusion
  114.8 0.7 reshape.50
  (2 shorter events, 0.0 us)
Async XLA Ops:
  0.6 32.2 %collective-permute-start = (bf16[256,768]{1,0:T(8,128)(2,1)}, bf16[256,768]{1,0:T(8,128)(2,1)S(1)}, u32[]{:S(2)}, u32[]{:S(2)}) collective-permute-start(bf16[256,768]{1,0:T(8,128)(2,1)} %text_ref.1), channel_id=1, source_target_pairs={{2,0},{3,1},{4,2},{5,3},{6,4},{7,5},{8,6},{9,7},{10,8},{11,9},{12,... | collective-permute-start | bytes 1179656 | tf_op jit(solution)/shard_map/ppermute | solution.py:24
  24.5 17.2 %collective-permute-start.1 = (bf16[256,768]{1,0:T(8,128)(2,1)}, bf16[256,768]{1,0:T(8,128)(2,1)S(1)}, u32[]{:S(2)}, u32[]{:S(2)}) collective-permute-start(bf16[256,768]{1,0:T(8,128)(2,1)} %text_ref.1), channel_id=1, source_target_pairs={{1022,0},{1023,1},{0,2},{1,3},{2,4},{3,5},{4,6},{5,7},{6,8},{7,9},... | collective-permute-start | bytes 1179656 | tf_op jit(solution)/shard_map/ppermute | solution.py:24
  26.4 19.8 %collective-permute-start.3 = (bf16[256,768]{1,0:T(8,128)(2,1)}, bf16[256,768]{1,0:T(8,128)(2,1)S(1)}, u32[]{:S(2)}, u32[]{:S(2)}) collective-permute-start(bf16[256,768]{1,0:T(8,128)(2,1)} %text_ref.1), channel_id=1, source_target_pairs={{0,1},{1,0},{2,3},{3,2},{4,5},{5,4},{6,7},{7,6},{8,9},{9,8},{10,11... | collective-permute-start | bytes 1179656 | tf_op jit(solution)/shard_map/ppermute | solution.py:28
  29.3 1.3 %copy-start = (bf16[768,768]{1,0:T(8,128)(2,1)S(1)}, bf16[768,768]{1,0:T(8,128)(2,1)}, u32[]{:S(2)}) copy-start(bf16[768,768]{1,0:T(8,128)(2,1)} %refs_2_.1) | copy-start | bytes 3538948
  30.6 1.0 copy-start.2
  31.6 0.7 copy-start.4
  32.3 14.0 %copy-start.5 = (bf16[256,768]{1,0:T(8,128)(2,1)S(1)}, bf16[256,768]{1,0:T(8,128)(2,1)}, u32[]{:S(2)}) copy-start(bf16[256,768]{1,0:T(8,128)(2,1)} %text_ref.1) | copy-start | bytes 1179652
  42.5 6.2 %collective-permute-start.2 = (bf16[256,768]{1,0:T(8,128)(2,1)}, bf16[256,768]{1,0:T(8,128)(2,1)S(1)}, u32[]{:S(2)}, u32[]{:S(2)}) collective-permute-start(bf16[256,768]{1,0:T(8,128)(2,1)} %broadcast_select_fusion.1), channel_id=1, source_target_pairs={{0,1},{1,0},{2,3},{3,2},{4,5},{5,4},{6,7},{7,6},{8,9},{9,8},{10,11... | collective-permute-start | bytes 1179656 | tf_op jit(solution)/shard_map/ppermute | solution.py:28
  46.3 2.5 %copy-start.3 = (bf16[256,768]{1,0:T(8,128)(2,1)S(1)}, bf16[256,768]{1,0:T(8,128)(2,1)}, u32[]{:S(2)}) copy-start(bf16[256,768]{1,0:T(8,128)(2,1)} %feats_ref.1) | copy-start | bytes 1179652
  51.4 12.6 %copy-start.1 = (bf16[768,768]{1,0:T(8,128)(2,1)S(1)}, bf16[768,768]{1,0:T(8,128)(2,1)}, u32[]{:S(2)}) copy-start(bf16[768,768]{1,0:T(8,128)(2,1)} %refs_2_.1) | copy-start | bytes 3538948
  51.4 29.7 %all-to-all-start = ((bf16[16,48,768]{2,1,0:T(8,128)(2,1)}), bf16[16,48,768]{2,1,0:T(8,128)(2,1)}, u32[]{:S(2)}, u32[]{:S(2)}) async-start(bf16[16,48,768]{2,1,0:T(8,128)(2,1)} %bitcast.4), calls=%async_computation | async-start | bytes 2359296 | tf_op jit(solution)/shard_map/all_to_all | solution.py:171
  55.9 49.8 %collective-permute-start.5 = (bf16[272,768]{1,0:T(8,128)(2,1)S(1)}, bf16[272,768]{1,0:T(8,128)(2,1)S(1)}, u32[]{:S(2)}, u32[]{:S(2)}) collective-permute-start(bf16[272,768]{1,0:T(8,128)(2,1)S(1)} %get-tuple-element.26.parcel_ref.own_ref), channel_id=1, source_target_pairs={{2,0},{3,1},{4,2},{5,3},{6,4},{7,5},{8,6},{9,7},{10,8},{11,9},{12,... | collective-permute-start | bytes 1253384 | tf_op jit(solution)/shard_map/ppermute | solution.py:24
  59.6 46.1 %collective-permute-start.6 = (bf16[272,768]{1,0:T(8,128)(2,1)S(1)}, bf16[272,768]{1,0:T(8,128)(2,1)S(1)}, u32[]{:S(2)}, u32[]{:S(2)}) collective-permute-start(bf16[272,768]{1,0:T(8,128)(2,1)S(1)} %get-tuple-element.26.parcel_ref.own_ref), channel_id=1, source_target_pairs={{1022,0},{1023,1},{0,2},{1,3},{2,4},{3,5},{4,6},{5,7},{6,8},{7,9},... | collective-permute-start | bytes 1253384 | tf_op jit(solution)/shard_map/ppermute | solution.py:24
  61.5 48.6 %collective-permute-start.4 = (bf16[272,768]{1,0:T(8,128)(2,1)S(1)}, bf16[272,768]{1,0:T(8,128)(2,1)S(1)}, u32[]{:S(2)}, u32[]{:S(2)}) collective-permute-start(bf16[272,768]{1,0:T(8,128)(2,1)S(1)} %get-tuple-element.26.parcel_ref.own_ref), channel_id=1, source_target_pairs={{0,1},{1,0},{2,3},{3,2},{4,5},{5,4},{6,7},{7,6},{8,9},{9,8},{10,11... | collective-permute-start | bytes 1253384 | tf_op jit(solution)/shard_map/ppermute | solution.py:28
  82.8 28.6 %copy-start.6 = (bf16[256,768]{1,0:T(8,128)(2,1)S(1)}, bf16[256,768]{1,0:T(8,128)(2,1)}, u32[]{:S(2)}) copy-start(bf16[256,768]{1,0:T(8,128)(2,1)} %text_ref.1) | copy-start | bytes 1179652
  83.9 30.7 %all-to-all-start.1 = ((bf16[64,2,288]{2,1,0:T(2,128)(2,1)}), bf16[64,2,288]{2,1,0:T(2,128)(2,1)S(1)}, u32[]{:S(2)}, u32[]{:S(2)}) async-start(bf16[64,2,288]{2,1,0:T(2,128)(2,1)} %reshape.49), calls=%async_computation.1 | async-start | bytes 196608 | tf_op jit(solution)/shard_map/all_to_all | solution.py:186
  105.7 5.7 %collective-permute-start.7 = (bf16[272,768]{1,0:T(8,128)(2,1)S(1)}, bf16[272,768]{1,0:T(8,128)(2,1)S(1)}, u32[]{:S(2)}, u32[]{:S(2)}) collective-permute-start(bf16[272,768]{1,0:T(8,128)(2,1)S(1)} %broadcast_select_fusion), channel_id=1, source_target_pairs={{0,1},{1,0},{2,3},{3,2},{4,5},{5,4},{6,7},{7,6},{8,9},{9,8},{10,11... | collective-permute-start | bytes 1253384 | tf_op jit(solution)/shard_map/ppermute | solution.py:28
